TPU v7x, 32 devices: a whole 2x2x4 slice. The times are simulated.
32 devices in a mesh: tm: 16 (over z, y, x), chan: 2 (over core).
Axes of the slice: x: 2, y: 2, z: 4, core: 2. Of those that a mesh axis runs over, the one named last changes fastest.
Arguments:
- strain: bfloat16 [128, 131072], P('chan', 'tm'), as said below
- fir_taps: float32 [128, 64], P('chan'), may hold values from -0.75 to 0.75
Outputs:
- factor: float32 [1024, 1024], P(('tm', 'chan'))
- whitened: bfloat16 [1024, 16384], P(None, ('tm', 'chan'))
Inputs may be any that keep to these rules, and one draw needn't show every extreme that they name: strain-rate samples of 128 channels.
All inputs are finite; a program needn't handle non-finite values.
Results may differ from a plain program's by a relative error of at most 0.001.
The roundings to bfloat16 on the way count: a program that leaves them out, or rounds other values in their place, can miss the bound.
Values may be sent and summed in bfloat16 or wider, within the bound.
A program may use at most 128 MiB of HBM per device.

v0:
```python
import functools

import jax
import jax.numpy as jnp
from jax import lax
from jax.experimental import pallas as pl
from jax.experimental.pallas import tpu as pltpu
from jax.sharding import PartitionSpec as P

LAGS = 8
TAPS = 64
STRIDE = 8
LANES = 128
MESH = pl.DeviceIdType.MESH
HIGHEST = lax.Precision.HIGHEST
VMEM = pl.BlockSpec(memory_space=pltpu.VMEM)


def shifted(value, axis, steps):
    count = lax.axis_size(axis)
    initial, last = (max(0, -steps), min(count, count - steps))
    return lax.ppermute(value, axis, [(source, source + steps) for source in range(initial, last)])


def decimate_kernel(strain_ref, rim_ref, taps_ref, out_ref, phase_ref):
    channels, samples = strain_ref.shape
    out_rows = samples // STRIDE
    width = STRIDE * LANES
    sample = lax.broadcasted_iota(jnp.int32, (width, width), 0)
    column = lax.broadcasted_iota(jnp.int32, (width, width), 1)
    wanted = STRIDE * (column % LANES) + column // LANES
    select = jnp.where(sample == wanted, 1.0, 0.0).astype(jnp.bfloat16)
    for g in range(out_rows // LANES + 1):
        if g < out_rows // LANES:
            part = jnp.dot(strain_ref[:, g * width : (g + 1) * width], select, preferred_element_type=jnp.float32)
        else:
            part = jnp.dot(rim_ref[...], select[:LANES], preferred_element_type=jnp.float32)
        for s in range(STRIDE):
            phase_ref[s, :, g * LANES : (g + 1) * LANES] = part[:, s * LANES : (s + 1) * LANES]
    span = out_rows + LANES
    for c in range(0, channels, 16):
        rows = slice(c, c + 16)
        total = jnp.zeros((16, span), jnp.float32)
        for j in range(TAPS // STRIDE):
            term = jnp.zeros((16, span), jnp.float32)
            for s in range(STRIDE):
                k = j * STRIDE + s
                term += taps_ref[rows, k : k + 1] * phase_ref[s, rows, :]
            total += term if j == 0 else pltpu.roll(term, span - j, 1)
        out_ref[rows, :] = total.astype(jnp.bfloat16)


def decimate(strain, rim, taps):
    channels, samples = strain.shape
    span = samples // STRIDE + LANES
    return pl.pallas_call(
        decimate_kernel,
        out_shape=jax.ShapeDtypeStruct((channels, span), jnp.bfloat16),
        in_specs=[VMEM] * 3,
        out_specs=VMEM,
        scratch_shapes=[pltpu.VMEM((STRIDE, channels, span), jnp.float32)],
        compiler_params=pltpu.CompilerParams(vmem_limit_bytes=40 * 2**20),
    )(strain, rim, taps)


def hankel_kernel(rows_ref, hankel_ref, sums_ref):
    group, first = lax.axis_index("tm"), lax.axis_index("chan")
    channels = rows_ref.shape[0]
    count = hankel_ref.shape[1]
    start = pl.multiple_of(first * count, LANES)
    window = rows_ref[:, pl.ds(start, count + LANES)].astype(jnp.float32)
    span = count + LANES
    for i in range(LAGS):
        moved = window if i == 0 else pltpu.roll(window, span - i, 1)
        hankel_ref[i * channels : (i + 1) * channels, :] = moved[:, :count].astype(jnp.bfloat16)
    leads = jnp.logical_and(group == 0, first == 0)
    skip = jnp.where(leads, LAGS - 1, 0)
    keep = lax.broadcasted_iota(jnp.int32, (channels, count), 1) >= skip
    left = jnp.where(keep, window[:, :count], 0.0).astype(jnp.bfloat16)
    sums_ref[:, : LAGS * channels] = lax.dot_general(
        left, hankel_ref[...], (((1,), (1,)), ((), ())), preferred_element_type=jnp.float32
    )
    lane = lax.broadcasted_iota(jnp.int32, (channels, LANES), 1)
    seen = jnp.where(leads, 2 * LAGS, 0)
    sums_ref[:, LAGS * channels :] = jnp.where(lane < seen, window[:, :LANES], 0.0)


def hankel_and_sums(rows, count):
    channels = rows.shape[0]
    return pl.pallas_call(
        hankel_kernel,
        out_shape=(
            jax.ShapeDtypeStruct((LAGS * channels, count), jnp.bfloat16),
            jax.ShapeDtypeStruct((channels, LAGS * channels + LANES), jnp.float32),
        ),
        in_specs=[VMEM],
        out_specs=(VMEM, VMEM),
        compiler_params=pltpu.CompilerParams(vmem_limit_bytes=40 * 2**20),
    )(rows)


def sum_kernel(near, mine_ref, out_ref, total, from_core, from_near, from_far, full, core_sem, near_sem, far_sem, all_sem, hand_sem):
    tm, chan = lax.axis_index("tm"), lax.axis_index("chan")
    far = lax.axis_size("tm") // near
    spot, place = lax.rem(tm, near), lax.div(tm, near)
    rows = mine_ref.shape[0]
    half = rows // 2
    piece = half // near
    core = {"chan": 1 - chan}

    def near_of(d):
        return lax.rem(spot + d, near)

    def near_id(d):
        return {"tm": place * near + near_of(d)}

    def far_id(d):
        return {"tm": lax.rem(place + d, far) * near + spot}

    def copy(source, target, sems, slot, device):
        return pltpu.make_async_remote_copy(
            src_ref=source,
            dst_ref=target,
            send_sem=sems.at[0, slot],
            recv_sem=sems.at[1, slot],
            device_id=device,
            device_id_type=MESH,
        )

    barrier = pltpu.get_barrier_semaphore()
    partners = [core] + [near_id(d) for d in range(1, near)] + [far_id(d) for d in range(1, far)]
    for partner in partners:
        pl.semaphore_signal(barrier, inc=1, device_id=partner, device_id_type=MESH)
    pl.semaphore_wait(barrier, len(partners))

    away = pl.ds(pl.multiple_of((1 - chan) * half, half), half)
    home = pl.ds(pl.multiple_of(chan * half, half), half)
    step = copy(mine_ref.at[away], from_core, core_sem, 0, core)
    step.start()
    step.wait()
    total[...] = mine_ref[home] + from_core[...]

    steps = []
    for d in range(1, near):
        part = total.at[pl.ds(pl.multiple_of(near_of(d) * piece, piece), piece)]
        steps.append(copy(part, from_near.at[d - 1], near_sem, d - 1, near_id(d)))
        steps[-1].start()
    own = total[pl.ds(pl.multiple_of(spot * piece, piece), piece)]
    for d in range(1, near):
        steps[d - 1].wait()
        own += from_near[d - 1]

    from_far[place] = own
    steps = []
    for d in range(1, far):
        steps.append(copy(from_far.at[place], from_far.at[place], far_sem, d - 1, far_id(d)))
        steps[-1].start()
    for step in steps:
        step.wait()
    own = from_far[0]
    for d in range(1, far):
        own += from_far[d]

    def at(spot_of):
        return pl.ds(pl.multiple_of(chan * half + spot_of * piece, piece), piece)

    full[at(spot)] = own
    steps = []
    for d in range(1, near):
        steps.append(copy(full.at[at(spot)], full.at[at(spot)], all_sem, d - 1, near_id(d)))
        steps[-1].start()
    hands = [copy(full.at[at(spot)], full.at[at(spot)], hand_sem, 0, core)]
    hands[0].start()
    for d in range(1, near):
        steps[d - 1].wait()
        came = at(lax.rem(spot - d + near, near))
        hands.append(copy(full.at[came], full.at[came], hand_sem, d, core))
        hands[-1].start()
    for hand in hands:
        hand.wait()
    out_ref[...] = full[...]


def summed(value):
    rows, columns = value.shape
    tm = lax.axis_size("tm")
    near = 4 if tm % 4 == 0 else 2
    far = tm // near
    half, piece = rows // 2, rows // 2 // near
    dtype = jnp.float32
    return pl.pallas_call(
        functools.partial(sum_kernel, near),
        out_shape=jax.ShapeDtypeStruct((rows, columns), dtype),
        in_specs=[VMEM],
        out_specs=VMEM,
        scratch_shapes=[
            pltpu.VMEM((half, columns), dtype),
            pltpu.VMEM((half, columns), dtype),
            pltpu.VMEM((near - 1, piece, columns), dtype),
            pltpu.VMEM((far, piece, columns), dtype),
            pltpu.VMEM((rows, columns), dtype),
            pltpu.SemaphoreType.DMA((2, 1)),
            pltpu.SemaphoreType.DMA((2, near - 1)),
            pltpu.SemaphoreType.DMA((2, max(far - 1, 1))),
            pltpu.SemaphoreType.DMA((2, near - 1)),
            pltpu.SemaphoreType.DMA((2, near)),
        ],
        compiler_params=pltpu.CompilerParams(
            collective_id=0, has_side_effects=True, vmem_limit_bytes=24 * 2**20
        ),
    )(value)


def factor_block(block):
    size = block.shape[0]
    row_id = lax.broadcasted_iota(jnp.int32, (size, size), 0)
    col_id = lax.broadcasted_iota(jnp.int32, (size, size), 1)
    sub = lax.broadcasted_iota(jnp.int32, (8, size), 0)
    low = block
    inv = jnp.where(row_id == col_id, 1.0, 0.0)
    factors, inverses = [], []
    for b in range(size // 8):
        cols = [jnp.broadcast_to(low[:, 8 * b + j : 8 * b + j + 1], low.shape) for j in range(8)]
        top, low = low[:8], low[8:]
        x_top, inv = inv[:8], inv[8:]
        c_top, c_low = [c[:8] for c in cols], [c[8:] for c in cols]
        scale = jnp.zeros((8, size), jnp.float32)
        more = b < size // 8 - 1
        for i in range(8):
            root = lax.rsqrt(jnp.broadcast_to(c_top[i][i : i + 1], (8, size)))
            over = root[:1] * root[:1]
            scale = jnp.where(sub == i, root, scale)
            below = jnp.where(sub > i, c_top[i], 0.0)
            row, x_row = top[i : i + 1] * over, x_top[i : i + 1] * over
            c_row = [c_top[j][i : i + 1] * over for j in range(i + 1, 8)]
            top, x_top = top - below * row, x_top - below * x_row
            for j in range(i + 1, 8):
                c_top[j] = c_top[j] - below * c_row[j - i - 1]
            if more:
                low, inv = low - c_low[i] * row, inv - c_low[i] * x_row
                for j in range(i + 1, 8):
                    c_low[j] = c_low[j] - c_low[i] * c_row[j - i - 1]
        factors.append(top * scale)
        inverses.append(x_top * scale)
    factor = jnp.concatenate(factors, axis=0)
    return jnp.where(col_id >= row_id, factor, 0.0), jnp.concatenate(inverses, axis=0)


def whiten_kernel(rows_all, sums_ref, hankel_ref, factor_ref, white_ref, work_ref, left_ref, right_ref):
    columns, count = hankel_ref.shape
    channels = columns // LAGS
    size = channels
    head = sums_ref[:, columns:]
    lane = lax.broadcasted_iota(jnp.int32, (channels, LANES), 1)
    heads = [(head if i == 0 else pltpu.roll(head, LANES - i, 1)).astype(jnp.bfloat16) for i in range(LAGS)]
    head_hankel = jnp.concatenate(heads, axis=0)
    scale = 1.0 / rows_all
    for i in range(LAGS):
        wide = columns - i * channels
        own = jnp.logical_and(lane >= i, lane < LAGS - 1)
        left = jnp.where(own, head, 0.0).astype(jnp.bfloat16)
        extra = lax.dot_general(
            left, head_hankel[:wide], (((1,), (1,)), ((), ())), preferred_element_type=jnp.float32
        )
        work_ref[i * channels : (i + 1) * channels, i * channels : columns] = (sums_ref[:, :wide] + extra) * scale
        if i:
            work_ref[i * channels : (i + 1) * channels, : i * channels] = jnp.zeros((channels, i * channels), jnp.float32)
    work_ref[:, columns:] = hankel_ref[...].astype(jnp.float32)

    def step(k, _):
        first = pl.multiple_of(k * size, size)
        mine = pl.ds(first, size)
        factor, inverse = factor_block(work_ref[mine, mine])
        solved = jnp.dot(inverse, work_ref[mine, :], preferred_element_type=jnp.float32, precision=HIGHEST)
        work_ref[mine, :] = solved
        work_ref[mine, mine] = factor
        white_ref[mine, :] = solved[:, columns:].astype(jnp.bfloat16)

        high = solved.astype(jnp.bfloat16)
        rest = solved - high.astype(jnp.float32)
        middle = rest.astype(jnp.bfloat16)
        little = (rest - middle.astype(jnp.float32)).astype(jnp.bfloat16)
        for n, (left, right) in enumerate(
            ((high, high), (high, middle), (middle, high), (middle, middle), (high, little), (little, high))
        ):
            left_ref[n * size : (n + 1) * size, :] = left[:, :columns]
            right_ref[n * size : (n + 1) * size, :] = right

        def update(start, i, _):
            other = pl.ds(pl.multiple_of(i * size, size), size)
            work_ref[other, start:] -= lax.dot_general(
                left_ref[:, other],
                right_ref[:, start:],
                (((0,), (0,)), ((), ())),
                preferred_element_type=jnp.float32,
            )
            return 0

        for q in range(0, LAGS, 2):
            initial, last = jnp.maximum(k + 1, q), jnp.maximum(k + 1, q + 2)
            lax.fori_loop(initial, last, functools.partial(update, q * size), 0)
        return 0

    lax.fori_loop(0, LAGS, step, 0)
    kept = factor_ref.shape[0]
    me = lax.axis_index("tm") * lax.axis_size("chan") + lax.axis_index("chan")
    first_row = pl.multiple_of(me * (columns // (lax.axis_size("tm") * lax.axis_size("chan"))) // kept * kept, kept)
    rows = work_ref[pl.ds(first_row, kept), :columns]
    row_id = lax.broadcasted_iota(jnp.int32, rows.shape, 0) + first_row
    col_id = lax.broadcasted_iota(jnp.int32, rows.shape, 1)
    factor_ref[...] = jnp.where(col_id >= row_id, rows, 0.0)


def whiten(sums, hankel, rows_all, kept):
    columns, count = hankel.shape
    return pl.pallas_call(
        functools.partial(whiten_kernel, rows_all),
        out_shape=(
            jax.ShapeDtypeStruct((kept, columns), jnp.float32),
            jax.ShapeDtypeStruct((columns, count), jnp.bfloat16),
        ),
        in_specs=[VMEM, VMEM],
        out_specs=(VMEM, VMEM),
        scratch_shapes=[
            pltpu.VMEM((columns, columns + count), jnp.float32),
            pltpu.VMEM((6 * columns // LAGS, columns), jnp.bfloat16),
            pltpu.VMEM((6 * columns // LAGS, columns + count), jnp.bfloat16),
        ],
        compiler_params=pltpu.CompilerParams(vmem_limit_bytes=48 * 2**20),
    )(sums, hankel)


def local(strain, fir_taps):
    samples = strain.shape[1]
    out_rows = samples // STRIDE
    rim = shifted(strain[:, :LANES], "tm", -1)
    decimated = decimate(strain, rim, fir_taps)
    gathered = lax.all_gather(decimated, "chan", axis=0, tiled=True)
    row_count = out_rows // lax.axis_size("chan")
    hankel, sums = hankel_and_sums(gathered, row_count)
    sums = summed(sums)
    devices_all = lax.axis_size(("tm", "chan"))
    columns = hankel.shape[0]
    factor_rows = columns // devices_all
    kept = max(8, factor_rows)
    factor, whitened = whiten(sums, hankel, row_count * devices_all, kept)
    if kept > factor_rows:
        first_row = lax.axis_index(("tm", "chan")) * factor_rows % kept
        factor = lax.dynamic_slice_in_dim(factor, first_row, factor_rows, 0)
    return (factor, whitened)


def solution(mesh):
    placed = (P("chan", "tm"), P("chan", None))
    return jax.shard_map(
        local,
        mesh=mesh,
        in_specs=placed,
        out_specs=(P(("tm", "chan"), None), P(None, ("tm", "chan"))),
        check_vma=False,
    )
```

profile of v0, /device:TPU:9, one launch (start us, length us, event | category | flops | bytes accessed | tf_op | source)
XLA Modules:
  0.0 100.9 jit_solution(8896548324422320221)
XLA Ops:
  0.6 0.0 copy-start.1
  0.6 0.7 slice.3
  1.4 3.9 %collective-permute-start = (bf16[64,128]{1,0:T(8,128)(2,1)S(1)}, bf16[64,128]{1,0:T(8,128)(2,1)S(1)}, u32[]{:S(2)}, u32[]{:S(2)}) collective-permute-start(bf16[64,128]{1,0:T(8,128)(2,1)S(1)} %slice.3), channel_id=1, source_target_pairs={{2,0},{4,2},{6,4},{8,6},{10,8},{12,10},{14,12},{16,14},{18,16},{20... | collective-permute-start | bytes 49160 | tf_op jit(solution)/shard_map/ppermute | solution.py:22
  5.3 0.8 collective-permute-done.rim_ref
  6.2 0.0 copy-done.1
  6.2 0.0 copy-start
  6.2 1.2 %copy-done = bf16[64,8192]{1,0:T(8,128)(2,1)S(1)} copy-done((bf16[64,8192]{1,0:T(8,128)(2,1)S(1)}, bf16[64,8192]{1,0:T(8,128)(2,1)}, u32[]{:S(2)}) %copy-start) | copy-done | bytes 1048600
  7.4 3.7 %shard_map.41 = bf16[64,1152]{1,0:T(8,128)(2,1)S(1)} custom-call(bf16[64,8192]{1,0:T(8,128)(2,1)S(1)} %copy-done, bf16[64,128]{1,0:T(8,128)(2,1)S(1)} %collective-permute-done.rim_ref, f32[64,64]{1,0:T(8,128)S(1)} %copy-done.1), custom_call_target="tpu_custom_call" | custom-call | tf_op jit(solution)/shard_map/pallas_call | solution.py:56
  11.1 3.2 %all_gather.3.rows_ref = bf16[128,1152]{1,0:T(8,128)(2,1)S(1)} all-gather(bf16[64,1152]{1,0:T(8,128)(2,1)S(1)} %shard_map.41), channel_id=1, replica_groups=mesh['tm'=16,'chan'=2] {'chan'}, dimensions={0}, use_global_device_ids=true | all-gather | bytes 442368 | tf_op jit(solution)/shard_map/all_gather | solution.py:338
  14.3 0.6 shard_map.42
  14.8 26.1 %shard_map.43.sums_ref = f32[128,1152]{1,0:T(8,128)S(1)} custom-call(f32[128,1152]{1,0:T(8,128)S(1)} %get-tuple-element.4.mine_ref), custom_call_target="tpu_custom_call" | custom-call | tf_op jit(solution)/shard_map/pallas_call | solution.py:191
  40.9 60.0 %shard_map.44 = (f32[32,1024]{1,0:T(8,128)}, bf16[1024,512]{1,0:T(8,128)(2,1)}) custom-call(f32[128,1152]{1,0:T(8,128)S(1)} %shard_map.43.sums_ref, bf16[1024,512]{1,0:T(8,128)(2,1)S(1)} %get-tuple-element.5.hankel_ref), custom_call_target="tpu_custom_call" | custom-call | tf_op jit(solution)/shard_map/pallas_call | solution.py:316
Async XLA Ops:
  0.6 5.5 %copy-start.1 = (f32[64,64]{1,0:T(8,128)S(1)}, f32[64,64]{1,0:T(8,128)}, u32[]{:S(2)}) copy-start(f32[64,64]{1,0:T(8,128)} %taps_ref.1) | copy-start | bytes 49156
  1.4 4.8 %collective-permute-start = (bf16[64,128]{1,0:T(8,128)(2,1)S(1)}, bf16[64,128]{1,0:T(8,128)(2,1)S(1)}, u32[]{:S(2)}, u32[]{:S(2)}) collective-permute-start(bf16[64,128]{1,0:T(8,128)(2,1)S(1)} %slice.3), channel_id=1, source_target_pairs={{2,0},{4,2},{6,4},{8,6},{10,8},{12,10},{14,12},{16,14},{18,16},{20... | collective-permute-start | bytes 49160 | tf_op jit(solution)/shard_map/ppermute | solution.py:22
  6.2 1.2 %copy-start = (bf16[64,8192]{1,0:T(8,128)(2,1)S(1)}, bf16[64,8192]{1,0:T(8,128)(2,1)}, u32[]{:S(2)}) copy-start(bf16[64,8192]{1,0:T(8,128)(2,1)} %strain_ref.1) | copy-start | bytes 3145732
where the time goes:
time: 102 us; the launch traced here: 101 us
  Pallas kernels  90.3 us (89%)
  starting transfers between devices  3.95 us (4%)
  blocking collectives  3.18 us (3%)
  local copies, waits for them, and re-layouts  1.95 us (2%)
    pallas_call x1, Pallas kernels, whiten(): pl.pallas_call(functools.partial(whiten_kernel, rows_all), out_shape=(jax...  60 us
    pallas_call x1, Pallas kernels, summed(): pl.pallas_call(functools.partial(sum_kernel, near), out_shape=jax.ShapeDt...  26.1 us
    ppermute x1, starting transfers between devices, shifted(): lax.ppermute(value, axis, [(source, source + steps) for source in range(i...  3.95 us
    pallas_call x1, Pallas kernels, decimate(): pl.pallas_call(decimate_kernel, out_shape=jax.ShapeDtypeStruct((channels,...  3.67 us
    all_gather x1, blocking collectives, local(): gathered = lax.all_gather(decimated, 'chan', axis=0, tiled=True)  3.18 us
  transfers between devices with their start and end apart: 1, of which 1 were waited for; matrix products, arithmetic and copies ran while one was open for 0% of the time, Pallas kernels for 0%

commit v1 on v0

--- a/solution.py
+++ b/solution.py
@@ -211,39 +211,85 @@
     )(value)
 
 
-def factor_block(block):
-    size = block.shape[0]
-    row_id = lax.broadcasted_iota(jnp.int32, (size, size), 0)
-    col_id = lax.broadcasted_iota(jnp.int32, (size, size), 1)
-    sub = lax.broadcasted_iota(jnp.int32, (8, size), 0)
-    low = block
-    inv = jnp.where(row_id == col_id, 1.0, 0.0)
-    factors, inverses = [], []
-    for b in range(size // 8):
-        cols = [jnp.broadcast_to(low[:, 8 * b + j : 8 * b + j + 1], low.shape) for j in range(8)]
-        top, low = low[:8], low[8:]
-        x_top, inv = inv[:8], inv[8:]
-        c_top, c_low = [c[:8] for c in cols], [c[8:] for c in cols]
-        scale = jnp.zeros((8, size), jnp.float32)
-        more = b < size // 8 - 1
-        for i in range(8):
-            root = lax.rsqrt(jnp.broadcast_to(c_top[i][i : i + 1], (8, size)))
-            over = root[:1] * root[:1]
-            scale = jnp.where(sub == i, root, scale)
-            below = jnp.where(sub > i, c_top[i], 0.0)
-            row, x_row = top[i : i + 1] * over, x_top[i : i + 1] * over
-            c_row = [c_top[j][i : i + 1] * over for j in range(i + 1, 8)]
-            top, x_top = top - below * row, x_top - below * x_row
-            for j in range(i + 1, 8):
-                c_top[j] = c_top[j] - below * c_row[j - i - 1]
-            if more:
-                low, inv = low - c_low[i] * row, inv - c_low[i] * x_row
-                for j in range(i + 1, 8):
-                    c_low[j] = c_low[j] - c_low[i] * c_row[j - i - 1]
-        factors.append(top * scale)
-        inverses.append(x_top * scale)
-    factor = jnp.concatenate(factors, axis=0)
-    return jnp.where(col_id >= row_id, factor, 0.0), jnp.concatenate(inverses, axis=0)
+GROUP = 16
+
+
+def split(value):
+    high = value.astype(jnp.bfloat16)
+    rest = value - high.astype(jnp.float32)
+    middle = rest.astype(jnp.bfloat16)
+    return high, middle, (rest - middle.astype(jnp.float32)).astype(jnp.bfloat16)
+
+
+def at(parts, i):
+    return jnp.broadcast_to(parts[i // 8][i % 8 : i % 8 + 1], parts[0].shape)
+
+
+def total_of(terms):
+    while len(terms) > 1:
+        terms = [sum(terms[m : m + 2]) for m in range(0, len(terms), 2)]
+    return terms[0]
+
+
+def factor_inverse(block):
+    n = block.shape[0]
+    high = GROUP // 8
+    rows = [block[8 * r : 8 * r + 8] for r in range(n // 8)]
+    sub = lax.broadcasted_iota(jnp.int32, (8, n), 0)
+    lane = lax.broadcasted_iota(jnp.int32, (8, n), 1)
+    out = []
+    for base in range(0, n // 8, high):
+        first = 8 * base
+
+        def col(value, j):
+            return jnp.broadcast_to(value[:, first + j : first + j + 1], (8, n))
+
+        cols = [[col(rows[base + v], j) for v in range(high)] for j in range(GROUP)]
+        inside = (lane >= first) & (lane < first + GROUP)
+        top = [
+            jnp.where(inside, jnp.where(lane == first + 8 * v + sub, 1.0, 0.0), rows[base + v]) for v in range(high)
+        ]
+        normal = [jnp.zeros((8, n), jnp.float32)] * high
+        for a in range(0, GROUP, 2):
+            b, v_of = a + 1, a // 8
+            is_a, is_b = sub == a % 8, sub == b % 8
+            col_a, col_b = cols[a], cols[b]
+            p, q, s = at(col_a, a), at(col_a, b), at(col_b, b)
+            det = p * s - q * q
+            over = 1.0 / det
+            top_a, top_b = at(top, a), at(top, b)
+            row_a = top_a * lax.rsqrt(p)
+            row_b = (p * top_b - q * top_a) * lax.rsqrt(p * det)
+            normal[v_of] = jnp.where(is_a, row_a, jnp.where(is_b, row_b, normal[v_of]))
+            less_a = [col_a[v] - jnp.where(is_a, 1.0, 0.0) if v == v_of else col_a[v] for v in range(high)]
+            less_b = [col_b[v] - jnp.where(is_b, 1.0, 0.0) if v == v_of else col_b[v] for v in range(high)]
+            by_a = [(s * less_a[v] - q * less_b[v]) * over for v in range(high)]
+            by_b = [(p * less_b[v] - q * less_a[v]) * over for v in range(high)]
+            for j in range(b + 1, GROUP):
+                x_a, x_b = at(cols[j], a), at(cols[j], b)
+                cols[j] = [cols[j][v] - by_a[v] * x_a - by_b[v] * x_b for v in range(high)]
+            top = [top[v] - by_a[v] * top_a - by_b[v] * top_b for v in range(high)]
+        out += [jnp.where(lane < first + GROUP, x, 0.0) for x in normal]
+        rest = list(range(base + high, n // 8))
+        spread = [at(top, j) for j in range(GROUP)]
+        for r in rest[:high]:
+            terms = [col(rows[r], j) * spread[j] for j in range(GROUP)]
+            rows[r] = jnp.where(inside, 0.0, rows[r]) - total_of(terms)
+        rest = rest[high:]
+        if rest:
+            left = jnp.concatenate([jnp.where(inside, rows[r], 0.0) for r in rest], axis=0)
+            before = [jnp.zeros((8, n), jnp.float32)] * base
+            after = [jnp.zeros((8, n), jnp.float32)] * (n // 8 - base - high)
+            l0, l1, l2 = split(left)
+            r0, r1, r2 = split(jnp.concatenate(before + top + after, axis=0))
+            update = jnp.dot(
+                jnp.concatenate([l0, l0, l1, l1, l0, l2], axis=1),
+                jnp.concatenate([r0, r1, r0, r1, r2, r0], axis=0),
+                preferred_element_type=jnp.float32,
+            )
+            for i, r in enumerate(rest):
+                rows[r] = jnp.where(inside, 0.0, rows[r]) - update[8 * i : 8 * i + 8]
+    return jnp.concatenate(out, axis=0)
 
 
 def whiten_kernel(rows_all, sums_ref, hankel_ref, factor_ref, white_ref, work_ref, left_ref, right_ref):
@@ -262,27 +308,31 @@
         extra = lax.dot_general(
             left, head_hankel[:wide], (((1,), (1,)), ((), ())), preferred_element_type=jnp.float32
         )
-        work_ref[i * channels : (i + 1) * channels, i * channels : columns] = (sums_ref[:, :wide] + extra) * scale
+        part = (sums_ref[:, :wide] + extra) * scale
+        if i == 0:
+            eye = lax.broadcasted_iota(jnp.int32, (size, size), 0) == lax.broadcasted_iota(jnp.int32, (size, size), 1)
+            diagonal = jnp.where(eye, part[:, :size], 0.0)
+            square = jnp.sum(diagonal, axis=0, keepdims=True)
+            down, across = lax.rsqrt(jnp.sum(diagonal, axis=1, keepdims=True)), lax.rsqrt(square)
+        part = part * down * jnp.concatenate([across] * (LAGS - i), axis=1)
+        work_ref[i * channels : (i + 1) * channels, i * channels : columns] = part
         if i:
             work_ref[i * channels : (i + 1) * channels, : i * channels] = jnp.zeros((channels, i * channels), jnp.float32)
-    work_ref[:, columns:] = hankel_ref[...].astype(jnp.float32)
+    for i in range(LAGS):
+        work_ref[i * channels : (i + 1) * channels, columns:] = (
+            hankel_ref[i * channels : (i + 1) * channels, :].astype(jnp.float32) * down
+        )
 
     def step(k, _):
         first = pl.multiple_of(k * size, size)
         mine = pl.ds(first, size)
-        factor, inverse = factor_block(work_ref[mine, mine])
+        inverse = factor_inverse(work_ref[mine, mine])
         solved = jnp.dot(inverse, work_ref[mine, :], preferred_element_type=jnp.float32, precision=HIGHEST)
         work_ref[mine, :] = solved
-        work_ref[mine, mine] = factor
         white_ref[mine, :] = solved[:, columns:].astype(jnp.bfloat16)
 
-        high = solved.astype(jnp.bfloat16)
-        rest = solved - high.astype(jnp.float32)
-        middle = rest.astype(jnp.bfloat16)
-        little = (rest - middle.astype(jnp.float32)).astype(jnp.bfloat16)
-        for n, (left, right) in enumerate(
-            ((high, high), (high, middle), (middle, high), (middle, middle), (high, little), (little, high))
-        ):
+        high, middle, _ = split(solved)
+        for n, (left, right) in enumerate(((high, high), (high, middle), (middle, high), (middle, middle))):
             left_ref[n * size : (n + 1) * size, :] = left[:, :columns]
             right_ref[n * size : (n + 1) * size, :] = right
 
@@ -308,7 +358,8 @@
     rows = work_ref[pl.ds(first_row, kept), :columns]
     row_id = lax.broadcasted_iota(jnp.int32, rows.shape, 0) + first_row
     col_id = lax.broadcasted_iota(jnp.int32, rows.shape, 1)
-    factor_ref[...] = jnp.where(col_id >= row_id, rows, 0.0)
+    back = jnp.concatenate([square * across] * LAGS, axis=1)
+    factor_ref[...] = jnp.where(col_id >= row_id, rows * back, 0.0)
 
 
 def whiten(sums, hankel, rows_all, kept):
@@ -323,8 +374,8 @@
         out_specs=(VMEM, VMEM),
         scratch_shapes=[
             pltpu.VMEM((columns, columns + count), jnp.float32),
-            pltpu.VMEM((6 * columns // LAGS, columns), jnp.bfloat16),
-            pltpu.VMEM((6 * columns // LAGS, columns + count), jnp.bfloat16),
+            pltpu.VMEM((4 * columns // LAGS, columns), jnp.bfloat16),
+            pltpu.VMEM((4 * columns // LAGS, columns + count), jnp.bfloat16),
         ],
         compiler_params=pltpu.CompilerParams(vmem_limit_bytes=48 * 2**20),
     )(sums, hankel)

time: 102 us -> 81.1 us (0.80)
  Pallas kernels: 90.3 us -> 69.9 us
    pallas_call x1, Pallas kernels: 60 us -> 39.6 us  [whiten(): pl.pallas_call(functools.partial(whiten_kernel, rows_all), out_shape=(jax...]
where the time goes in v1:
time: 81.1 us; the launch traced here: 80.5 us
  Pallas kernels  69.9 us (86%)
  starting transfers between devices  3.95 us (5%)
  blocking collectives  3.18 us (4%)
  local copies, waits for them, and re-layouts  1.95 us (2%)
  waiting for transfers between devices  0.85 us (1%)
    pallas_call x1, Pallas kernels, whiten(): pl.pallas_call(functools.partial(whiten_kernel, rows_all), out_shape=(jax...  39.6 us
    pallas_call x1, Pallas kernels, summed(): pl.pallas_call(functools.partial(sum_kernel, near), out_shape=jax.ShapeDt...  26.1 us
    ppermute x1, starting transfers between devices, shifted(): lax.ppermute(value, axis, [(source, source + steps) for source in range(i...  3.95 us
    pallas_call x1, Pallas kernels, decimate(): pl.pallas_call(decimate_kernel, out_shape=jax.ShapeDtypeStruct((channels,...  3.67 us
    all_gather x1, blocking collectives, local(): gathered = lax.all_gather(decimated, 'chan', axis=0, tiled=True)  3.18 us
  transfers between devices with their start and end apart: 1, of which 1 were waited for; matrix products, arithmetic and copies ran while one was open for 0% of the time, Pallas kernels for 0%

profile of v1, /device:TPU:9, one launch (start us, length us, event | category | flops | bytes accessed | tf_op | source)
XLA Modules:
  0.0 80.5 jit_solution(18219922900947031791)
XLA Ops:
  0.6 0.0 copy-start.1
  0.6 0.7 slice.3
  1.4 3.9 %collective-permute-start = (bf16[64,128]{1,0:T(8,128)(2,1)S(1)}, bf16[64,128]{1,0:T(8,128)(2,1)S(1)}, u32[]{:S(2)}, u32[]{:S(2)}) collective-permute-start(bf16[64,128]{1,0:T(8,128)(2,1)S(1)} %slice.3), channel_id=1, source_target_pairs={{2,0},{4,2},{6,4},{8,6},{10,8},{12,10},{14,12},{16,14},{18,16},{20... | collective-permute-start | bytes 49160 | tf_op jit(solution)/shard_map/ppermute | solution.py:22
  5.3 0.8 %collective-permute-done.rim_ref = bf16[64,128]{1,0:T(8,128)(2,1)S(1)} collective-permute-done((bf16[64,128]{1,0:T(8,128)(2,1)S(1)}, bf16[64,128]{1,0:T(8,128)(2,1)S(1)}, u32[]{:S(2)}, u32[]{:S(2)}) %collective-permute-start) | collective-permute-done | bytes 16416 | tf_op jit(solution)/shard_map/ppermute | solution.py:22
  6.2 0.0 copy-done.1
  6.2 0.0 copy-start
  6.2 1.2 %copy-done = bf16[64,8192]{1,0:T(8,128)(2,1)S(1)} copy-done((bf16[64,8192]{1,0:T(8,128)(2,1)S(1)}, bf16[64,8192]{1,0:T(8,128)(2,1)}, u32[]{:S(2)}) %copy-start) | copy-done | bytes 1048600
  7.4 3.7 %shard_map.41 = bf16[64,1152]{1,0:T(8,128)(2,1)S(1)} custom-call(bf16[64,8192]{1,0:T(8,128)(2,1)S(1)} %copy-done, bf16[64,128]{1,0:T(8,128)(2,1)S(1)} %collective-permute-done.rim_ref, f32[64,64]{1,0:T(8,128)S(1)} %copy-done.1), custom_call_target="tpu_custom_call" | custom-call | tf_op jit(solution)/shard_map/pallas_call | solution.py:56
  11.1 3.2 %all_gather.3.rows_ref = bf16[128,1152]{1,0:T(8,128)(2,1)S(1)} all-gather(bf16[64,1152]{1,0:T(8,128)(2,1)S(1)} %shard_map.41), channel_id=1, replica_groups=mesh['tm'=16,'chan'=2] {'chan'}, dimensions={0}, use_global_device_ids=true | all-gather | bytes 442368 | tf_op jit(solution)/shard_map/all_gather | solution.py:389
  14.3 0.6 shard_map.42
  14.8 26.1 %shard_map.43.sums_ref = f32[128,1152]{1,0:T(8,128)S(1)} custom-call(f32[128,1152]{1,0:T(8,128)S(1)} %get-tuple-element.4.mine_ref), custom_call_target="tpu_custom_call" | custom-call | tf_op jit(solution)/shard_map/pallas_call | solution.py:191
  40.9 39.6 %shard_map.44 = (f32[32,1024]{1,0:T(8,128)}, bf16[1024,512]{1,0:T(8,128)(2,1)}) custom-call(f32[128,1152]{1,0:T(8,128)S(1)} %shard_map.43.sums_ref, bf16[1024,512]{1,0:T(8,128)(2,1)S(1)} %get-tuple-element.5.hankel_ref), custom_call_target="tpu_custom_call" | custom-call | tf_op jit(solution)/shard_map/pallas_call | solution.py:367
Async XLA Ops:
  0.6 5.5 %copy-start.1 = (f32[64,64]{1,0:T(8,128)S(1)}, f32[64,64]{1,0:T(8,128)}, u32[]{:S(2)}) copy-start(f32[64,64]{1,0:T(8,128)} %taps_ref.1) | copy-start | bytes 49156
  1.4 4.8 %collective-permute-start = (bf16[64,128]{1,0:T(8,128)(2,1)S(1)}, bf16[64,128]{1,0:T(8,128)(2,1)S(1)}, u32[]{:S(2)}, u32[]{:S(2)}) collective-permute-start(bf16[64,128]{1,0:T(8,128)(2,1)S(1)} %slice.3), channel_id=1, source_target_pairs={{2,0},{4,2},{6,4},{8,6},{10,8},{12,10},{14,12},{16,14},{18,16},{20... | collective-permute-start | bytes 49160 | tf_op jit(solution)/shard_map/ppermute | solution.py:22
  6.2 1.2 %copy-start = (bf16[64,8192]{1,0:T(8,128)(2,1)S(1)}, bf16[64,8192]{1,0:T(8,128)(2,1)}, u32[]{:S(2)}) copy-start(bf16[64,8192]{1,0:T(8,128)(2,1)} %strain_ref.1) | copy-start | bytes 3145732

commit v2 on v1

--- a/solution.py
+++ b/solution.py
@@ -231,7 +231,7 @@
     return terms[0]
 
 
-def factor_inverse(block):
+def factor_inverse(block, jobs):
     n = block.shape[0]
     high = GROUP // 8
     rows = [block[8 * r : 8 * r + 8] for r in range(n // 8)]
@@ -246,6 +246,8 @@
 
         cols = [[col(rows[base + v], j) for v in range(high)] for j in range(GROUP)]
         inside = (lane >= first) & (lane < first + GROUP)
+        if jobs:
+            jobs.pop(0)()
         top = [
             jnp.where(inside, jnp.where(lane == first + 8 * v + sub, 1.0, 0.0), rows[base + v]) for v in range(high)
         ]
@@ -292,10 +294,23 @@
     return jnp.concatenate(out, axis=0)
 
 
-def whiten_kernel(rows_all, sums_ref, hankel_ref, factor_ref, white_ref, work_ref, left_ref, right_ref):
+def matmul(left, right, over=1):
+    return lax.dot_general(left, right, (((over,), (0,)), ((), ())), preferred_element_type=jnp.float32)
+
+
+def halves(value):
+    high = value.astype(jnp.bfloat16)
+    return high, (value - high.astype(jnp.float32)).astype(jnp.bfloat16)
+
+
+def whiten_kernel(
+    rows_all, sums_ref, hankel_ref, factor_ref, white_ref, work_ref, high_ref, mid_ref, turned_ref, part_ref, block_ref
+):
     columns, count = hankel_ref.shape
     channels = columns // LAGS
     size = channels
+    width = 2 * size
+    total = columns + count
     head = sums_ref[:, columns:]
     lane = lax.broadcasted_iota(jnp.int32, (channels, LANES), 1)
     heads = [(head if i == 0 else pltpu.roll(head, LANES - i, 1)).astype(jnp.bfloat16) for i in range(LAGS)]
@@ -315,43 +330,71 @@
             square = jnp.sum(diagonal, axis=0, keepdims=True)
             down, across = lax.rsqrt(jnp.sum(diagonal, axis=1, keepdims=True)), lax.rsqrt(square)
         part = part * down * jnp.concatenate([across] * (LAGS - i), axis=1)
+        if i == 0:
+            block_ref[...] = part[:, :size]
         work_ref[i * channels : (i + 1) * channels, i * channels : columns] = part
-        if i:
-            work_ref[i * channels : (i + 1) * channels, : i * channels] = jnp.zeros((channels, i * channels), jnp.float32)
-    for i in range(LAGS):
         work_ref[i * channels : (i + 1) * channels, columns:] = (
             hankel_ref[i * channels : (i + 1) * channels, :].astype(jnp.float32) * down
         )
-
-    def step(k, _):
-        first = pl.multiple_of(k * size, size)
-        mine = pl.ds(first, size)
-        inverse = factor_inverse(work_ref[mine, mine])
-        solved = jnp.dot(inverse, work_ref[mine, :], preferred_element_type=jnp.float32, precision=HIGHEST)
-        work_ref[mine, :] = solved
-        white_ref[mine, :] = solved[:, columns:].astype(jnp.bfloat16)
-
-        high, middle, _ = split(solved)
-        for n, (left, right) in enumerate(((high, high), (high, middle), (middle, high), (middle, middle))):
-            left_ref[n * size : (n + 1) * size, :] = left[:, :columns]
-            right_ref[n * size : (n + 1) * size, :] = right
-
-        def update(start, i, _):
-            other = pl.ds(pl.multiple_of(i * size, size), size)
-            work_ref[other, start:] -= lax.dot_general(
-                left_ref[:, other],
-                right_ref[:, start:],
-                (((0,), (0,)), ((), ())),
-                preferred_element_type=jnp.float32,
+    near = columns // 2
+    turned_ref[...] = jnp.zeros(turned_ref.shape, jnp.bfloat16)
+    high_ref[:near] = jnp.zeros((near, total), jnp.bfloat16)
+    mid_ref[:near] = jnp.zeros((near, total), jnp.bfloat16)
+
+    def step(depth, initial, k, _):
+        mine = pl.ds(pl.multiple_of(k * size, size), size)
+        after = pl.ds(pl.multiple_of(jnp.minimum(k + 1, LAGS - 1) * size, size), size)
+        if depth < near:
+            far = pl.ds(pl.multiple_of(near + k * size, size), size)
+            high_ref[far] = jnp.zeros((size, total), jnp.bfloat16)
+            mid_ref[far] = jnp.zeros((size, total), jnp.bfloat16)
+        def prepare(n):
+            here = slice(n, n + width)
+            done = matmul(turned_ref[:, :depth], high_ref[:depth, here]) + matmul(
+                turned_ref[:, :depth], mid_ref[:depth, here]
             )
-            return 0
-
-        for q in range(0, LAGS, 2):
-            initial, last = jnp.maximum(k + 1, q), jnp.maximum(k + 1, q + 2)
-            lax.fori_loop(initial, last, functools.partial(update, q * size), 0)
+            high, mid = halves(work_ref[mine, here] - (done[:size] + done[size:]))
+            part_ref[:size, here] = high
+            part_ref[size:, here] = mid
+
+        def look_ahead():
+            turned_ref[:size, :depth] = high_ref[:depth, after].T
+            turned_ref[size:, :depth] = mid_ref[:depth, after].T
+            done = matmul(turned_ref[:, :depth], high_ref[:depth, after])
+            more = matmul(turned_ref[:, :depth], mid_ref[:depth, after])
+            return (done[:size] + more[size:]) + (done[size:] + more[:size])
+
+        seen = []
+        jobs = [functools.partial(prepare, n) for n in range(initial, total, width)]
+        jobs.append(lambda: seen.append(look_ahead()))
+        inverse = factor_inverse(block_ref[...], jobs)
+        seen = work_ref[after, after] - seen[0]
+
+        high, mid = halves(inverse)
+        left = jnp.concatenate(
+            [jnp.concatenate([high, high], axis=1), jnp.concatenate([mid, mid], axis=1)], axis=0
+        )
+        solved = matmul(left, part_ref[:, after])
+        pair = jnp.concatenate(halves(solved[:size] + solved[size:]), axis=1)
+        pair_turned = pair.T
+        turned_ref[:, mine] = pair_turned
+        square = matmul(pair_turned, pair)
+        block_ref[...] = seen - ((square[:size, :size] + square[size:, size:]) + (square[:size, size:] + square[size:, :size]))
+        for n in range(initial, total, width):
+            here = slice(n, n + width)
+            solved = matmul(left, part_ref[:, here])
+            solved = solved[:size] + solved[size:]
+            high, mid = halves(solved)
+            high_ref[mine, here] = high
+            mid_ref[mine, here] = mid
+            if n < columns:
+                work_ref[mine, here] = solved
+            else:
+                white_ref[mine, n - columns : n - columns + width] = solved.astype(jnp.bfloat16)
         return 0
 
-    lax.fori_loop(0, LAGS, step, 0)
+    lax.fori_loop(0, LAGS // 2, functools.partial(step, near - size, 0), 0)
+    lax.fori_loop(LAGS // 2, LAGS, functools.partial(step, columns - size, near), 0)
     kept = factor_ref.shape[0]
     me = lax.axis_index("tm") * lax.axis_size("chan") + lax.axis_index("chan")
     first_row = pl.multiple_of(me * (columns // (lax.axis_size("tm") * lax.axis_size("chan"))) // kept * kept, kept)
@@ -364,6 +407,7 @@
 
 def whiten(sums, hankel, rows_all, kept):
     columns, count = hankel.shape
+    size = columns // LAGS
     return pl.pallas_call(
         functools.partial(whiten_kernel, rows_all),
         out_shape=(
@@ -374,8 +418,11 @@
         out_specs=(VMEM, VMEM),
         scratch_shapes=[
             pltpu.VMEM((columns, columns + count), jnp.float32),
-            pltpu.VMEM((4 * columns // LAGS, columns), jnp.bfloat16),
-            pltpu.VMEM((4 * columns // LAGS, columns + count), jnp.bfloat16),
+            pltpu.VMEM((columns, columns + count), jnp.bfloat16),
+            pltpu.VMEM((columns, columns + count), jnp.bfloat16),
+            pltpu.VMEM((2 * size, columns), jnp.bfloat16),
+            pltpu.VMEM((2 * size, columns + count), jnp.bfloat16),
+            pltpu.VMEM((size, size), jnp.float32),
         ],
         compiler_params=pltpu.CompilerParams(vmem_limit_bytes=48 * 2**20),
     )(sums, hankel)

time: 81.1 us -> 71 us (0.88)
  Pallas kernels: 69.9 us -> 59.8 us
    pallas_call x1, Pallas kernels: 39.6 us -> 29.5 us  [whiten(): pl.pallas_call(functools.partial(whiten_kernel, rows_all), out_shape=(jax...]
where the time goes in v2:
time: 71 us; the launch traced here: 70.4 us
  Pallas kernels  59.8 us (84%)
  starting transfers between devices  3.95 us (6%)
  blocking collectives  3.18 us (4%)
  local copies, waits for them, and re-layouts  1.95 us (3%)
  waiting for transfers between devices  0.85 us (1%)
    pallas_call x1, Pallas kernels, whiten(): pl.pallas_call(functools.partial(whiten_kernel, rows_all), out_shape=(jax...  29.5 us
    pallas_call x1, Pallas kernels, summed(): pl.pallas_call(functools.partial(sum_kernel, near), out_shape=jax.ShapeDt...  26.1 us
    ppermute x1, starting transfers between devices, shifted(): lax.ppermute(value, axis, [(source, source + steps) for source in range(i...  3.95 us
    pallas_call x1, Pallas kernels, decimate(): pl.pallas_call(decimate_kernel, out_shape=jax.ShapeDtypeStruct((channels,...  3.67 us
    all_gather x1, blocking collectives, local(): gathered = lax.all_gather(decimated, 'chan', axis=0, tiled=True)  3.18 us
  transfers between devices with their start and end apart: 1, of which 1 were waited for; matrix products, arithmetic and copies ran while one was open for 0% of the time, Pallas kernels for 0%

profile of v2, /device:TPU:9, one launch (start us, length us, event | category | flops | bytes accessed | tf_op | source)
XLA Modules:
  0.0 70.4 jit_solution(7045499662337128581)
XLA Ops:
  0.6 0.0 copy-start.1
  0.6 0.7 %slice.3 = bf16[64,128]{1,0:T(8,128)(2,1)S(1)} slice(bf16[64,8192]{1,0:T(8,128)(2,1)} %strain_ref.1), slice={[0:64], [0:128]} | slice | bytes 32768 | tf_op jit(solution)/shard_map/slice | solution.py:434
  1.4 3.9 %collective-permute-start = (bf16[64,128]{1,0:T(8,128)(2,1)S(1)}, bf16[64,128]{1,0:T(8,128)(2,1)S(1)}, u32[]{:S(2)}, u32[]{:S(2)}) collective-permute-start(bf16[64,128]{1,0:T(8,128)(2,1)S(1)} %slice.3), channel_id=1, source_target_pairs={{2,0},{4,2},{6,4},{8,6},{10,8},{12,10},{14,12},{16,14},{18,16},{20... | collective-permute-start | bytes 49160 | tf_op jit(solution)/shard_map/ppermute | solution.py:22
  5.3 0.8 %collective-permute-done.rim_ref = bf16[64,128]{1,0:T(8,128)(2,1)S(1)} collective-permute-done((bf16[64,128]{1,0:T(8,128)(2,1)S(1)}, bf16[64,128]{1,0:T(8,128)(2,1)S(1)}, u32[]{:S(2)}, u32[]{:S(2)}) %collective-permute-start) | collective-permute-done | bytes 16416 | tf_op jit(solution)/shard_map/ppermute | solution.py:22
  6.2 0.0 copy-done.1
  6.2 0.0 copy-start
  6.2 1.2 %copy-done = bf16[64,8192]{1,0:T(8,128)(2,1)S(1)} copy-done((bf16[64,8192]{1,0:T(8,128)(2,1)S(1)}, bf16[64,8192]{1,0:T(8,128)(2,1)}, u32[]{:S(2)}) %copy-start) | copy-done | bytes 1048600
  7.4 3.7 %shard_map.41 = bf16[64,1152]{1,0:T(8,128)(2,1)S(1)} custom-call(bf16[64,8192]{1,0:T(8,128)(2,1)S(1)} %copy-done, bf16[64,128]{1,0:T(8,128)(2,1)S(1)} %collective-permute-done.rim_ref, f32[64,64]{1,0:T(8,128)S(1)} %copy-done.1), custom_call_target="tpu_custom_call" | custom-call | tf_op jit(solution)/shard_map/pallas_call | solution.py:56
  11.1 3.2 %all_gather.3.rows_ref = bf16[128,1152]{1,0:T(8,128)(2,1)S(1)} all-gather(bf16[64,1152]{1,0:T(8,128)(2,1)S(1)} %shard_map.41), channel_id=1, replica_groups=mesh['tm'=16,'chan'=2] {'chan'}, dimensions={0}, use_global_device_ids=true | all-gather | bytes 442368 | tf_op jit(solution)/shard_map/all_gather | solution.py:436
  14.3 0.6 shard_map.42
  14.8 26.1 %shard_map.43.sums_ref = f32[128,1152]{1,0:T(8,128)S(1)} custom-call(f32[128,1152]{1,0:T(8,128)S(1)} %get-tuple-element.4.mine_ref), custom_call_target="tpu_custom_call" | custom-call | tf_op jit(solution)/shard_map/pallas_call | solution.py:191
  40.9 29.5 %shard_map.44 = (f32[32,1024]{1,0:T(8,128)}, bf16[1024,512]{1,0:T(8,128)(2,1)}) custom-call(f32[128,1152]{1,0:T(8,128)S(1)} %shard_map.43.sums_ref, bf16[1024,512]{1,0:T(8,128)(2,1)S(1)} %get-tuple-element.5.hankel_ref), custom_call_target="tpu_custom_call" | custom-call | tf_op jit(solution)/shard_map/pallas_call | solution.py:411
Async XLA Ops:
  0.6 5.5 %copy-start.1 = (f32[64,64]{1,0:T(8,128)S(1)}, f32[64,64]{1,0:T(8,128)}, u32[]{:S(2)}) copy-start(f32[64,64]{1,0:T(8,128)} %taps_ref.1) | copy-start | bytes 49156
  1.4 4.8 %collective-permute-start = (bf16[64,128]{1,0:T(8,128)(2,1)S(1)}, bf16[64,128]{1,0:T(8,128)(2,1)S(1)}, u32[]{:S(2)}, u32[]{:S(2)}) collective-permute-start(bf16[64,128]{1,0:T(8,128)(2,1)S(1)} %slice.3), channel_id=1, source_target_pairs={{2,0},{4,2},{6,4},{8,6},{10,8},{12,10},{14,12},{16,14},{18,16},{20... | collective-permute-start | bytes 49160 | tf_op jit(solution)/shard_map/ppermute | solution.py:22
  6.2 1.2 %copy-start = (bf16[64,8192]{1,0:T(8,128)(2,1)S(1)}, bf16[64,8192]{1,0:T(8,128)(2,1)}, u32[]{:S(2)}) copy-start(bf16[64,8192]{1,0:T(8,128)(2,1)} %strain_ref.1) | copy-start | bytes 3145732

commit v3 on v2

--- a/solution.py
+++ b/solution.py
@@ -99,7 +99,7 @@
     )(rows)
 
 
-def sum_kernel(near, mine_ref, out_ref, total, from_core, from_near, from_far, full, core_sem, near_sem, far_sem, all_sem, hand_sem):
+def wide_sum_kernel(near, mine_ref, out_ref, total, from_core, from_near, from_far, full, core_sem, near_sem, far_sem, all_sem, hand_sem):
     tm, chan = lax.axis_index("tm"), lax.axis_index("chan")
     far = lax.axis_size("tm") // near
     spot, place = lax.rem(tm, near), lax.div(tm, near)
@@ -181,7 +181,7 @@
     out_ref[...] = full[...]
 
 
-def summed(value):
+def wide_summed(value):
     rows, columns = value.shape
     tm = lax.axis_size("tm")
     near = 4 if tm % 4 == 0 else 2
@@ -189,7 +189,7 @@
     half, piece = rows // 2, rows // 2 // near
     dtype = jnp.float32
     return pl.pallas_call(
-        functools.partial(sum_kernel, near),
+        functools.partial(wide_sum_kernel, near),
         out_shape=jax.ShapeDtypeStruct((rows, columns), dtype),
         in_specs=[VMEM],
         out_specs=VMEM,
@@ -209,6 +209,221 @@
             collective_id=0, has_side_effects=True, vmem_limit_bytes=24 * 2**20
         ),
     )(value)
+
+
+def phases(part, phase_ref, g):
+    for s in range(STRIDE):
+        phase_ref[s, :, g * LANES : (g + 1) * LANES] = part[:, s * LANES : (s + 1) * LANES]
+
+
+def selection():
+    width = STRIDE * LANES
+    sample = lax.broadcasted_iota(jnp.int32, (width, width), 0)
+    column = lax.broadcasted_iota(jnp.int32, (width, width), 1)
+    wanted = STRIDE * (column % LANES) + column // LANES
+    return jnp.where(sample == wanted, 1.0, 0.0).astype(jnp.bfloat16)
+
+
+def taps_applied(rows, taps_ref, phase_ref):
+    span = phase_ref.shape[2]
+    total = jnp.zeros((16, span), jnp.float32)
+    for j in range(TAPS // STRIDE):
+        term = jnp.zeros((16, span), jnp.float32)
+        for s in range(STRIDE):
+            k = j * STRIDE + s
+            term += taps_ref[rows, k : k + 1] * phase_ref[s, rows, :]
+        total += term if j == 0 else pltpu.roll(term, span - j, 1)
+    return total.astype(jnp.bfloat16)
+
+
+def front_kernel(
+    near, strain_ref, taps_ref, hankel_ref, out_ref,
+    raw, rim, phase_ref, both, mine_ref, total, from_core, from_near, own, from_far, full,
+    load_sem, rim_sem, both_sem, core_sem, near_sem, far_sem, spread_sem, all_sem, hand_sem,
+):
+    tm, chan = lax.axis_index("tm"), lax.axis_index("chan")
+    count_tm = lax.axis_size("tm")
+    far = count_tm // near
+    spot, place = lax.rem(tm, near), lax.div(tm, near)
+    core = {"chan": 1 - chan}
+    before, behind = {"tm": lax.rem(tm + count_tm - 1, count_tm)}, {"tm": lax.rem(tm + 1, count_tm)}
+
+    def near_of(d):
+        return lax.rem(spot + d, near)
+
+    def near_id(d):
+        return {"tm": place * near + near_of(d)}
+
+    def far_of(d):
+        return lax.rem(place + d, far)
+
+    def far_id(d):
+        return {"tm": far_of(d) * near + spot}
+
+    def block(first, count):
+        return pl.ds(pl.multiple_of(first, 8), count)
+
+    def copy(source, target, sems, slot, device):
+        step = pltpu.make_async_remote_copy(
+            src_ref=source,
+            dst_ref=target,
+            send_sem=sems.at[0, slot],
+            recv_sem=sems.at[1, slot],
+            device_id=device,
+            device_id_type=MESH,
+        )
+        step.start()
+        return step
+
+    channels, samples = raw.shape
+    width = STRIDE * LANES
+    groups = samples // width
+    loads = []
+    for g in range(groups):
+        there = (slice(None), slice(g * width, (g + 1) * width))
+        loads.append(pltpu.make_async_copy(strain_ref.at[there], raw.at[there], load_sem.at[g]))
+        loads[-1].start()
+    barrier = pltpu.get_barrier_semaphore()
+    partners = [before, behind, core] + [near_id(d) for d in range(1, near)] + [far_id(d) for d in range(1, far)]
+    for partner in partners:
+        pl.semaphore_signal(barrier, inc=1, device_id=partner, device_id_type=MESH)
+    select = selection()
+    rim_step = None
+    for g in range(groups):
+        loads[g].wait()
+        if g == groups // 2:
+            pl.semaphore_wait(barrier, len(partners))
+            rim_step = copy(raw.at[:, :LANES], rim, rim_sem, 0, before)
+        part = jnp.dot(raw[:, g * width : (g + 1) * width], select, preferred_element_type=jnp.float32)
+        phases(part, phase_ref, g)
+    rim_step.wait()
+    last = jnp.where(tm == count_tm - 1, 0.0, rim[...].astype(jnp.float32)).astype(jnp.bfloat16)
+    phases(jnp.dot(last, select[:LANES], preferred_element_type=jnp.float32), phase_ref, groups)
+    for c in range(0, channels, 16):
+        both[chan, c : c + 16, :] = taps_applied(slice(c, c + 16), taps_ref, phase_ref)
+    step = copy(both.at[chan], both.at[chan], both_sem, 0, core)
+    step.wait()
+
+    size = 2 * channels
+    count = hankel_ref.shape[1]
+    span = count + LANES
+    start = pl.multiple_of(chan * count, LANES)
+    window = jnp.concatenate([both[0, :, pl.ds(start, span)], both[1, :, pl.ds(start, span)]], axis=0)
+    window = window.astype(jnp.float32)
+    for i in range(LAGS):
+        moved = window if i == 0 else pltpu.roll(window, span - i, 1)
+        hankel_ref[i * size : (i + 1) * size, :] = moved[:, :count].astype(jnp.bfloat16)
+    skip = jnp.where(jnp.logical_and(tm == 0, chan == 0), LAGS - 1, 0)
+    keep = lax.broadcasted_iota(jnp.int32, (size, count), 1) >= skip
+    left = jnp.where(keep, window[:, :count], 0.0).astype(jnp.bfloat16)
+    for i in range(LAGS):
+        mine_ref[i * size : (i + 1) * size, :] = lax.dot_general(
+            left,
+            hankel_ref[i * size : (i + 1) * size, :],
+            (((1,), (1,)), ((), ())),
+            preferred_element_type=jnp.float32,
+        )
+    head = jnp.concatenate([both[0, :, :LANES], both[1, :, :LANES]], axis=0).astype(jnp.float32).T
+    head = jnp.where(chan == 0, head[:8], head[8:16])
+
+    half = LAGS * size // 2
+    piece = half // near
+    sub = piece // far
+    pitch = sub + 8
+
+    def at_full(core_of, spot_of, place_of, rows):
+        return block(((core_of * near + spot_of) * far + place_of) * pitch, rows)
+
+    step = copy(mine_ref.at[block((1 - chan) * half, half)], from_core, core_sem, 0, core)
+    step.wait()
+    total[...] = mine_ref[block(chan * half, half)] + from_core[...]
+    steps = []
+    for d in range(1, near):
+        steps.append(copy(total.at[block(near_of(d) * piece, piece)], from_near.at[d - 1], near_sem, d - 1, near_id(d)))
+    value = total[block(spot * piece, piece)]
+    for d in range(1, near):
+        steps[d - 1].wait()
+        value += from_near[d - 1]
+    if far > 1:
+        own[...] = value
+        steps = []
+        for d in range(1, far):
+            steps.append(copy(own.at[block(far_of(d) * sub, sub)], from_far.at[d - 1], far_sem, d - 1, far_id(d)))
+        value = own[block(place * sub, sub)]
+        for d in range(1, far):
+            steps[d - 1].wait()
+            value += from_far[d - 1]
+    here = at_full(chan, spot, place, pitch)
+    full[here] = jnp.concatenate([value, head], axis=0)
+    steps = []
+    for d in range(1, far):
+        steps.append(copy(full.at[here], full.at[here], spread_sem, d - 1, far_id(d)))
+    for step in steps:
+        step.wait()
+    here = at_full(chan, spot, 0, far * pitch)
+    steps = []
+    for d in range(1, near):
+        steps.append(copy(full.at[here], full.at[here], all_sem, d - 1, near_id(d)))
+    for step in steps:
+        step.wait()
+    here = at_full(chan, 0, 0, near * far * pitch)
+    step = copy(full.at[here], full.at[here], hand_sem, 0, core)
+    step.wait()
+    for i in range(2 * near * far):
+        out_ref[i * sub : (i + 1) * sub, :] = full[i * pitch : i * pitch + sub, :]
+    there = near * far * pitch
+    ends = [full[sub : sub + 8, :], full[there + sub : there + sub + 8, :]]
+    ends.append(jnp.zeros((size - 16, size), jnp.float32))
+    out_ref[LAGS * size :, :] = jnp.concatenate(ends, axis=0).T
+
+
+def front(strain, taps):
+    channels, samples = strain.shape
+    size = 2 * channels
+    tm = lax.axis_size("tm")
+    near = tm
+    far = tm // near
+    half = LAGS * size // 2
+    piece = half // near
+    sub = piece // far
+    span = samples // STRIDE + LANES
+    dtype = jnp.float32
+    dma = pltpu.SemaphoreType.DMA
+    farther = max(far - 1, 1)
+    return pl.pallas_call(
+        functools.partial(front_kernel, near),
+        out_shape=(
+            jax.ShapeDtypeStruct((LAGS * size, samples // STRIDE // 2), jnp.bfloat16),
+            jax.ShapeDtypeStruct(((LAGS + 1) * size, size), dtype),
+        ),
+        in_specs=[pl.BlockSpec(memory_space=pltpu.HBM), VMEM],
+        out_specs=(VMEM, VMEM),
+        scratch_shapes=[
+            pltpu.VMEM((channels, samples), jnp.bfloat16),
+            pltpu.VMEM((channels, LANES), jnp.bfloat16),
+            pltpu.VMEM((STRIDE, channels, span), dtype),
+            pltpu.VMEM((2, channels, span), jnp.bfloat16),
+            pltpu.VMEM((LAGS * size, size), dtype),
+            pltpu.VMEM((half, size), dtype),
+            pltpu.VMEM((half, size), dtype),
+            pltpu.VMEM((near - 1, piece, size), dtype),
+            pltpu.VMEM((piece, size), dtype),
+            pltpu.VMEM((farther, sub, size), dtype),
+            pltpu.VMEM(((sub + 8) * 2 * near * far, size), dtype),
+            dma((samples // STRIDE // LANES,)),
+            dma((2, 1)),
+            dma((2, 1)),
+            dma((2, 1)),
+            dma((2, near - 1)),
+            dma((2, farther)),
+            dma((2, farther)),
+            dma((2, near - 1)),
+            dma((2, 1)),
+        ],
+        compiler_params=pltpu.CompilerParams(
+            collective_id=1, has_side_effects=True, vmem_limit_bytes=40 * 2**20
+        ),
+    )(strain, taps)
 
 
 GROUP = 16
@@ -311,7 +526,7 @@
     size = channels
     width = 2 * size
     total = columns + count
-    head = sums_ref[:, columns:]
+    head = sums_ref[columns:, :]
     lane = lax.broadcasted_iota(jnp.int32, (channels, LANES), 1)
     heads = [(head if i == 0 else pltpu.roll(head, LANES - i, 1)).astype(jnp.bfloat16) for i in range(LAGS)]
     head_hankel = jnp.concatenate(heads, axis=0)
@@ -323,16 +538,18 @@
         extra = lax.dot_general(
             left, head_hankel[:wide], (((1,), (1,)), ((), ())), preferred_element_type=jnp.float32
         )
-        part = (sums_ref[:, :wide] + extra) * scale
-        if i == 0:
-            eye = lax.broadcasted_iota(jnp.int32, (size, size), 0) == lax.broadcasted_iota(jnp.int32, (size, size), 1)
-            diagonal = jnp.where(eye, part[:, :size], 0.0)
-            square = jnp.sum(diagonal, axis=0, keepdims=True)
-            down, across = lax.rsqrt(jnp.sum(diagonal, axis=1, keepdims=True)), lax.rsqrt(square)
-        part = part * down * jnp.concatenate([across] * (LAGS - i), axis=1)
-        if i == 0:
-            block_ref[...] = part[:, :size]
-        work_ref[i * channels : (i + 1) * channels, i * channels : columns] = part
+        for j in range(LAGS - i):
+            there = slice(j * size, (j + 1) * size)
+            part = (sums_ref[there, :] + extra[:, there]) * scale
+            if i + j == 0:
+                eye = lax.broadcasted_iota(jnp.int32, part.shape, 0) == lax.broadcasted_iota(jnp.int32, part.shape, 1)
+                diagonal = jnp.where(eye, part, 0.0)
+                square = jnp.sum(diagonal, axis=0, keepdims=True)
+                down, across = lax.rsqrt(jnp.sum(diagonal, axis=1, keepdims=True)), lax.rsqrt(square)
+            part = part * down * across
+            if i + j == 0:
+                block_ref[...] = part
+            work_ref[i * size : (i + 1) * size, (i + j) * size : (i + j + 1) * size] = part
         work_ref[i * channels : (i + 1) * channels, columns:] = (
             hankel_ref[i * channels : (i + 1) * channels, :].astype(jnp.float32) * down
         )
@@ -428,15 +645,21 @@
     )(sums, hankel)
 
 
-def local(strain, fir_taps):
-    samples = strain.shape[1]
-    out_rows = samples // STRIDE
+def staged(strain, fir_taps):
+    out_rows = strain.shape[1] // STRIDE
     rim = shifted(strain[:, :LANES], "tm", -1)
     decimated = decimate(strain, rim, fir_taps)
     gathered = lax.all_gather(decimated, "chan", axis=0, tiled=True)
-    row_count = out_rows // lax.axis_size("chan")
-    hankel, sums = hankel_and_sums(gathered, row_count)
-    sums = summed(sums)
+    hankel, sums = hankel_and_sums(gathered, out_rows // lax.axis_size("chan"))
+    sums = wide_summed(sums)
+    return hankel, jnp.concatenate([sums[:, i : i + LANES] for i in range(0, sums.shape[1], LANES)], axis=0)
+
+
+def local(strain, fir_taps):
+    row_count = strain.shape[1] // STRIDE // lax.axis_size("chan")
+    tm = lax.axis_size("tm")
+    even = tm >= 8 and tm % 4 == 0 and LAGS * strain.shape[0] % (8 * tm) == 0
+    hankel, sums = (front if even else staged)(strain, fir_taps)
     devices_all = lax.axis_size(("tm", "chan"))
     columns = hankel.shape[0]
     factor_rows = columns // devices_all

time: 71 us -> 65.8 us (0.927)
  starting transfers between devices: 3.95 us -> 0 us
  Pallas kernels: 59.8 us -> 63 us
  blocking collectives: 3.18 us -> 0 us
  waiting for transfers between devices: 0.85 us -> 0 us
    ppermute x1 -> x0, starting transfers between devices: 3.95 us -> none  [shifted(): lax.ppermute(value, axis, [(source, source + steps) for source in range(i...]
    all_gather x1 -> x0, blocking collectives: 3.18 us -> none  [local(): gathered = lax.all_gather(decimated, 'chan', axis=0, tiled=True)]
    pallas_call x3 -> x1, Pallas kernels: 30.3 us -> 33.2 us  [front(): pl.pallas_call(functools.partial(front_kernel, near), out_shape=(jax.Shap...]
    ppermute x1 -> x0, waiting for transfers between devices: 0.85 us -> none  [shifted(): lax.ppermute(value, axis, [(source, source + steps) for source in range(i...]
    unnamed x4, local copies, waits for them, and re-layouts: 1.23 us -> 1.98 us
    slice x1 -> x0, local copies, waits for them, and re-layouts: 0.73 us -> none  [local(): rim = shifted(strain[:, :LANES], 'tm', -1)]
  transfers between devices with their start and end apart: 1 -> 0, of which waited for: 1 -> 0; matrix products, arithmetic and copies ran while one was open for 0% -> 0% of each run, Pallas kernels for 0% -> 0%
where the time goes in v3:
time: 65.8 us; the launch traced here: 65.6 us
  Pallas kernels  63 us (96%)
  local copies, waits for them, and re-layouts  1.98 us (3%)
    pallas_call x1, Pallas kernels, front(): pl.pallas_call(functools.partial(front_kernel, near), out_shape=(jax.Shap...  33.2 us
    pallas_call x1, Pallas kernels, whiten(): pl.pallas_call(functools.partial(whiten_kernel, rows_all), out_shape=(jax...  29.7 us
    unnamed x4, local copies, waits for them, and re-layouts  1.98 us

profile of v3, /device:TPU:9, one launch (start us, length us, event | category | flops | bytes accessed | tf_op | source)
XLA Modules:
  0.0 65.6 jit_solution(204736799086151818)
XLA Ops:
  0.6 0.0 copy-start
  0.6 1.2 %copy-done = bf16[64,8192]{1,0:T(8,128)(2,1)S(1)} copy-done((bf16[64,8192]{1,0:T(8,128)(2,1)S(1)}, bf16[64,8192]{1,0:T(8,128)(2,1)}, u32[]{:S(2)}) %copy-start) | copy-done | bytes 1048600
  1.9 0.0 copy-start.1
  1.9 0.8 %copy-done.1 = f32[64,64]{1,0:T(8,128)S(1)} copy-done((f32[64,64]{1,0:T(8,128)S(1)}, f32[64,64]{1,0:T(8,128)}, u32[]{:S(2)}) %copy-start.1) | copy-done | bytes 16408
  2.6 33.2 %shard_map.41 = (bf16[1024,512]{1,0:T(8,128)(2,1)S(1)}, f32[1152,128]{1,0:T(8,128)S(1)}) custom-call(bf16[64,8192]{1,0:T(8,128)(2,1)S(1)} %copy-done, f32[64,64]{1,0:T(8,128)S(1)} %copy-done.1), custom_call_target="tpu_custom_call" | custom-call | tf_op jit(solution)/shard_map/pallas_call | solution.py:393
  35.9 29.7 %shard_map.42 = (f32[32,1024]{1,0:T(8,128)}, bf16[1024,512]{1,0:T(8,128)(2,1)}) custom-call(f32[1152,128]{1,0:T(8,128)S(1)} %get-tuple-element.4.sums_ref, bf16[1024,512]{1,0:T(8,128)(2,1)S(1)} %get-tuple-element.5.hankel_ref), custom_call_target="tpu_custom_call" | custom-call | tf_op jit(solution)/shard_map/pallas_call | solution.py:628
Async XLA Ops:
  0.6 1.2 %copy-start = (bf16[64,8192]{1,0:T(8,128)(2,1)S(1)}, bf16[64,8192]{1,0:T(8,128)(2,1)}, u32[]{:S(2)}) copy-start(bf16[64,8192]{1,0:T(8,128)(2,1)} %strain_ref.1) | copy-start | bytes 3145732
  1.9 0.8 %copy-start.1 = (f32[64,64]{1,0:T(8,128)S(1)}, f32[64,64]{1,0:T(8,128)}, u32[]{:S(2)}) copy-start(f32[64,64]{1,0:T(8,128)} %taps_ref.1) | copy-start | bytes 49156

commit v4 on v3

--- a/solution.py
+++ b/solution.py
@@ -224,22 +224,22 @@
     return jnp.where(sample == wanted, 1.0, 0.0).astype(jnp.bfloat16)
 
 
-def taps_applied(rows, taps_ref, phase_ref):
-    span = phase_ref.shape[2]
+def taps_applied(rows, lanes, taps_ref, phase_ref):
+    span = lanes.stop - lanes.start
     total = jnp.zeros((16, span), jnp.float32)
     for j in range(TAPS // STRIDE):
         term = jnp.zeros((16, span), jnp.float32)
         for s in range(STRIDE):
             k = j * STRIDE + s
-            term += taps_ref[rows, k : k + 1] * phase_ref[s, rows, :]
+            term += taps_ref[rows, k : k + 1] * phase_ref[s, rows, lanes]
         total += term if j == 0 else pltpu.roll(term, span - j, 1)
     return total.astype(jnp.bfloat16)
 
 
 def front_kernel(
     near, strain_ref, taps_ref, hankel_ref, out_ref,
-    raw, rim, phase_ref, both, mine_ref, total, from_core, from_near, own, from_far, full,
-    load_sem, rim_sem, both_sem, core_sem, near_sem, far_sem, spread_sem, all_sem, hand_sem,
+    rim, phase_ref, both, total, from_near, own, from_far, full,
+    rim_sem, both_sem, near_sem, far_sem, spread_sem, all_sem, hand_sem,
 ):
     tm, chan = lax.axis_index("tm"), lax.axis_index("chan")
     count_tm = lax.axis_size("tm")
@@ -275,32 +275,27 @@
         step.start()
         return step
 
-    channels, samples = raw.shape
+    channels, samples = strain_ref.shape
     width = STRIDE * LANES
     groups = samples // width
-    loads = []
-    for g in range(groups):
-        there = (slice(None), slice(g * width, (g + 1) * width))
-        loads.append(pltpu.make_async_copy(strain_ref.at[there], raw.at[there], load_sem.at[g]))
-        loads[-1].start()
     barrier = pltpu.get_barrier_semaphore()
     partners = [before, behind, core] + [near_id(d) for d in range(1, near)] + [far_id(d) for d in range(1, far)]
     for partner in partners:
         pl.semaphore_signal(barrier, inc=1, device_id=partner, device_id_type=MESH)
     select = selection()
-    rim_step = None
     for g in range(groups):
-        loads[g].wait()
-        if g == groups // 2:
-            pl.semaphore_wait(barrier, len(partners))
-            rim_step = copy(raw.at[:, :LANES], rim, rim_sem, 0, before)
-        part = jnp.dot(raw[:, g * width : (g + 1) * width], select, preferred_element_type=jnp.float32)
-        phases(part, phase_ref, g)
+        here = slice(g * width, (g + 1) * width)
+        phases(jnp.dot(strain_ref[:, here], select, preferred_element_type=jnp.float32), phase_ref, g)
+    pl.semaphore_wait(barrier, len(partners))
+    rim_step = copy(strain_ref.at[:, :LANES], rim, rim_sem, 0, before)
+    inner, edge = slice(0, groups * LANES), slice((groups - 1) * LANES, (groups + 1) * LANES)
+    for c in range(0, channels, 16):
+        both[chan, c : c + 16, inner] = taps_applied(slice(c, c + 16), inner, taps_ref, phase_ref)
     rim_step.wait()
     last = jnp.where(tm == count_tm - 1, 0.0, rim[...].astype(jnp.float32)).astype(jnp.bfloat16)
     phases(jnp.dot(last, select[:LANES], preferred_element_type=jnp.float32), phase_ref, groups)
     for c in range(0, channels, 16):
-        both[chan, c : c + 16, :] = taps_applied(slice(c, c + 16), taps_ref, phase_ref)
+        both[chan, c : c + 16, edge] = taps_applied(slice(c, c + 16), edge, taps_ref, phase_ref)
     step = copy(both.at[chan], both.at[chan], both_sem, 0, core)
     step.wait()
 
@@ -313,13 +308,16 @@
     for i in range(LAGS):
         moved = window if i == 0 else pltpu.roll(window, span - i, 1)
         hankel_ref[i * size : (i + 1) * size, :] = moved[:, :count].astype(jnp.bfloat16)
-    skip = jnp.where(jnp.logical_and(tm == 0, chan == 0), LAGS - 1, 0)
-    keep = lax.broadcasted_iota(jnp.int32, (size, count), 1) >= skip
-    left = jnp.where(keep, window[:, :count], 0.0).astype(jnp.bfloat16)
-    for i in range(LAGS):
-        mine_ref[i * size : (i + 1) * size, :] = lax.dot_general(
+    rows = jnp.concatenate([both[0], both[1]], axis=0).astype(jnp.float32)
+    span = rows.shape[1]
+    keep = lax.broadcasted_iota(jnp.int32, (size, 2 * count), 1) >= jnp.where(tm == 0, LAGS - 1, 0)
+    left = jnp.where(keep, rows[:, : 2 * count], 0.0).astype(jnp.bfloat16)
+    first = jnp.where(chan == 0, rows, pltpu.roll(rows, span - LAGS // 2, 1))
+    for i in range(LAGS // 2):
+        moved = first if i == 0 else pltpu.roll(first, span - i, 1)
+        total[i * size : (i + 1) * size, :] = lax.dot_general(
             left,
-            hankel_ref[i * size : (i + 1) * size, :],
+            moved[:, : 2 * count].astype(jnp.bfloat16),
             (((1,), (1,)), ((), ())),
             preferred_element_type=jnp.float32,
         )
@@ -334,9 +332,6 @@
     def at_full(core_of, spot_of, place_of, rows):
         return block(((core_of * near + spot_of) * far + place_of) * pitch, rows)
 
-    step = copy(mine_ref.at[block((1 - chan) * half, half)], from_core, core_sem, 0, core)
-    step.wait()
-    total[...] = mine_ref[block(chan * half, half)] + from_core[...]
     steps = []
     for d in range(1, near):
         steps.append(copy(total.at[block(near_of(d) * piece, piece)], from_near.at[d - 1], near_sem, d - 1, near_id(d)))
@@ -396,22 +391,17 @@
             jax.ShapeDtypeStruct((LAGS * size, samples // STRIDE // 2), jnp.bfloat16),
             jax.ShapeDtypeStruct(((LAGS + 1) * size, size), dtype),
         ),
-        in_specs=[pl.BlockSpec(memory_space=pltpu.HBM), VMEM],
+        in_specs=[VMEM, VMEM],
         out_specs=(VMEM, VMEM),
         scratch_shapes=[
-            pltpu.VMEM((channels, samples), jnp.bfloat16),
             pltpu.VMEM((channels, LANES), jnp.bfloat16),
             pltpu.VMEM((STRIDE, channels, span), dtype),
             pltpu.VMEM((2, channels, span), jnp.bfloat16),
-            pltpu.VMEM((LAGS * size, size), dtype),
-            pltpu.VMEM((half, size), dtype),
             pltpu.VMEM((half, size), dtype),
             pltpu.VMEM((near - 1, piece, size), dtype),
             pltpu.VMEM((piece, size), dtype),
             pltpu.VMEM((farther, sub, size), dtype),
             pltpu.VMEM(((sub + 8) * 2 * near * far, size), dtype),
-            dma((samples // STRIDE // LANES,)),
-            dma((2, 1)),
             dma((2, 1)),
             dma((2, 1)),
             dma((2, near - 1)),
@@ -480,11 +470,15 @@
             normal[v_of] = jnp.where(is_a, row_a, jnp.where(is_b, row_b, normal[v_of]))
             less_a = [col_a[v] - jnp.where(is_a, 1.0, 0.0) if v == v_of else col_a[v] for v in range(high)]
             less_b = [col_b[v] - jnp.where(is_b, 1.0, 0.0) if v == v_of else col_b[v] for v in range(high)]
-            by_a = [(s * less_a[v] - q * less_b[v]) * over for v in range(high)]
-            by_b = [(p * less_b[v] - q * less_a[v]) * over for v in range(high)]
+            some_a = [s * less_a[v] - q * less_b[v] for v in range(high)]
+            some_b = [p * less_b[v] - q * less_a[v] for v in range(high)]
+            by_a, by_b = [x * over for x in some_a], [x * over for x in some_b]
             for j in range(b + 1, GROUP):
                 x_a, x_b = at(cols[j], a), at(cols[j], b)
-                cols[j] = [cols[j][v] - by_a[v] * x_a - by_b[v] * x_b for v in range(high)]
+                if j < b + 3:
+                    cols[j] = [cols[j][v] - (some_a[v] * x_a + some_b[v] * x_b) * over for v in range(high)]
+                else:
+                    cols[j] = [cols[j][v] - by_a[v] * x_a - by_b[v] * x_b for v in range(high)]
             top = [top[v] - by_a[v] * top_a - by_b[v] * top_b for v in range(high)]
         out += [jnp.where(lane < first + GROUP, x, 0.0) for x in normal]
         rest = list(range(base + high, n // 8))
@@ -519,7 +513,7 @@
 
 
 def whiten_kernel(
-    rows_all, sums_ref, hankel_ref, factor_ref, white_ref, work_ref, high_ref, mid_ref, turned_ref, part_ref, block_ref
+    rows_all, sums_ref, hankel_ref, factor_ref, white_ref, work_ref, pairs_ref, turned_ref, part_ref, block_ref
 ):
     columns, count = hankel_ref.shape
     channels = columns // LAGS
@@ -555,55 +549,65 @@
         )
     near = columns // 2
     turned_ref[...] = jnp.zeros(turned_ref.shape, jnp.bfloat16)
-    high_ref[:near] = jnp.zeros((near, total), jnp.bfloat16)
-    mid_ref[:near] = jnp.zeros((near, total), jnp.bfloat16)
+    pairs_ref[:columns] = jnp.zeros((columns, total), jnp.bfloat16)
+
+    def turn(j, high, mid):
+        for half in range(2):
+            lanes = pl.ds(pl.multiple_of((2 * j + half) * size, size), size)
+            turned_ref[:size, lanes] = high
+            turned_ref[size:, lanes] = mid
+
+    def product(deep, here):
+        done = matmul(turned_ref[:, :deep], pairs_ref[:deep, here])
+        return done[:size] + done[size:]
+
+    def small(left, right):
+        done = matmul(left, right)
+        return done[:size] + done[size:]
+
+    def stacked(high, mid):
+        return jnp.concatenate([jnp.concatenate([high, high], axis=1), jnp.concatenate([mid, mid], axis=1)], axis=0)
 
     def step(depth, initial, k, _):
         mine = pl.ds(pl.multiple_of(k * size, size), size)
-        after = pl.ds(pl.multiple_of(jnp.minimum(k + 1, LAGS - 1) * size, size), size)
+        later = jnp.minimum(k + 1, LAGS - 1)
+        after = pl.ds(pl.multiple_of(later * size, size), size)
+
         if depth < near:
-            far = pl.ds(pl.multiple_of(near + k * size, size), size)
-            high_ref[far] = jnp.zeros((size, total), jnp.bfloat16)
-            mid_ref[far] = jnp.zeros((size, total), jnp.bfloat16)
+            pairs_ref[pl.ds(pl.multiple_of(columns + 2 * k * size, size), 2 * size)] = jnp.zeros(
+                (2 * size, total), jnp.bfloat16
+            )
+
         def prepare(n):
             here = slice(n, n + width)
-            done = matmul(turned_ref[:, :depth], high_ref[:depth, here]) + matmul(
-                turned_ref[:, :depth], mid_ref[:depth, here]
-            )
-            high, mid = halves(work_ref[mine, here] - (done[:size] + done[size:]))
+            high, mid = halves(work_ref[mine, here] - product(2 * depth, here))
             part_ref[:size, here] = high
             part_ref[size:, here] = mid
 
+        seen = []
+
         def look_ahead():
-            turned_ref[:size, :depth] = high_ref[:depth, after].T
-            turned_ref[size:, :depth] = mid_ref[:depth, after].T
-            done = matmul(turned_ref[:, :depth], high_ref[:depth, after])
-            more = matmul(turned_ref[:, :depth], mid_ref[:depth, after])
-            return (done[:size] + more[size:]) + (done[size:] + more[:size])
-
-        seen = []
+            for j in range(depth // size):
+                first = 2 * j * size
+                turn(j, pairs_ref[first : first + size, after].T, pairs_ref[first + size : first + 2 * size, after].T)
+            seen.append(product(2 * depth, after))
+
         jobs = [functools.partial(prepare, n) for n in range(initial, total, width)]
-        jobs.append(lambda: seen.append(look_ahead()))
+        jobs.append(look_ahead)
         inverse = factor_inverse(block_ref[...], jobs)
         seen = work_ref[after, after] - seen[0]
 
-        high, mid = halves(inverse)
-        left = jnp.concatenate(
-            [jnp.concatenate([high, high], axis=1), jnp.concatenate([mid, mid], axis=1)], axis=0
-        )
-        solved = matmul(left, part_ref[:, after])
-        pair = jnp.concatenate(halves(solved[:size] + solved[size:]), axis=1)
-        pair_turned = pair.T
-        turned_ref[:, mine] = pair_turned
-        square = matmul(pair_turned, pair)
-        block_ref[...] = seen - ((square[:size, :size] + square[size:, size:]) + (square[:size, size:] + square[size:, :size]))
+        left = stacked(*halves(inverse))
+        high, mid = halves(small(left, part_ref[:, after]))
+        high_turned, mid_turned = high.T, mid.T
+        block_ref[...] = seen - small(stacked(high_turned, mid_turned), jnp.concatenate([high, mid], axis=0))
+        turn(k, high_turned, mid_turned)
         for n in range(initial, total, width):
             here = slice(n, n + width)
-            solved = matmul(left, part_ref[:, here])
-            solved = solved[:size] + solved[size:]
+            solved = small(left, part_ref[:, here])
             high, mid = halves(solved)
-            high_ref[mine, here] = high
-            mid_ref[mine, here] = mid
+            pairs_ref[pl.ds(pl.multiple_of(2 * k * size, size), size), here] = high
+            pairs_ref[pl.ds(pl.multiple_of((2 * k + 1) * size, size), size), here] = mid
             if n < columns:
                 work_ref[mine, here] = solved
             else:
@@ -635,9 +639,8 @@
         out_specs=(VMEM, VMEM),
         scratch_shapes=[
             pltpu.VMEM((columns, columns + count), jnp.float32),
-            pltpu.VMEM((columns, columns + count), jnp.bfloat16),
-            pltpu.VMEM((columns, columns + count), jnp.bfloat16),
-            pltpu.VMEM((2 * size, columns), jnp.bfloat16),
+            pltpu.VMEM((2 * columns, columns + count), jnp.bfloat16),
+            pltpu.VMEM((2 * size, 2 * columns), jnp.bfloat16),
             pltpu.VMEM((2 * size, columns + count), jnp.bfloat16),
             pltpu.VMEM((size, size), jnp.float32),
         ],

time: 65.8 us -> 63.9 us (0.971)
  Pallas kernels: 63 us -> 61.1 us
    pallas_call x1, Pallas kernels: 33.2 us -> 31.8 us  [front(): pl.pallas_call(functools.partial(front_kernel, near), out_shape=(jax.Shap...]
where the time goes in v4:
time: 63.9 us; the launch traced here: 63.7 us
  Pallas kernels  61.1 us (96%)
  local copies, waits for them, and re-layouts  1.98 us (3%)
  between operations  0.65 us (1%)
    pallas_call x1, Pallas kernels, front(): pl.pallas_call(functools.partial(front_kernel, near), out_shape=(jax.Shap...  31.8 us
    pallas_call x1, Pallas kernels, whiten(): pl.pallas_call(functools.partial(whiten_kernel, rows_all), out_shape=(jax...  29.3 us
    unnamed x4, local copies, waits for them, and re-layouts  1.98 us

profile of v4, /device:TPU:9, one launch (start us, length us, event | category | flops | bytes accessed | tf_op | source)
XLA Modules:
  0.0 63.7 jit_solution(10821212489960341929)
XLA Ops:
  0.6 0.0 copy-start
  0.6 1.2 %copy-done = bf16[64,8192]{1,0:T(8,128)(2,1)S(1)} copy-done((bf16[64,8192]{1,0:T(8,128)(2,1)S(1)}, bf16[64,8192]{1,0:T(8,128)(2,1)}, u32[]{:S(2)}) %copy-start) | copy-done | bytes 1048600
  1.9 0.0 copy-start.1
  1.9 0.8 %copy-done.1 = f32[64,64]{1,0:T(8,128)S(1)} copy-done((f32[64,64]{1,0:T(8,128)S(1)}, f32[64,64]{1,0:T(8,128)}, u32[]{:S(2)}) %copy-start.1) | copy-done | bytes 16408
  2.6 31.8 %shard_map.41 = (bf16[1024,512]{1,0:T(8,128)(2,1)S(1)}, f32[1152,128]{1,0:T(8,128)S(1)}) custom-call(bf16[64,8192]{1,0:T(8,128)(2,1)S(1)} %copy-done, f32[64,64]{1,0:T(8,128)S(1)} %copy-done.1), custom_call_target="tpu_custom_call" | custom-call | tf_op jit(solution)/shard_map/pallas_call | solution.py:388
  34.4 29.3 %shard_map.42 = (f32[32,1024]{1,0:T(8,128)}, bf16[1024,512]{1,0:T(8,128)(2,1)}) custom-call(f32[1152,128]{1,0:T(8,128)S(1)} %get-tuple-element.4.sums_ref, bf16[1024,512]{1,0:T(8,128)(2,1)S(1)} %get-tuple-element.5.hankel_ref), custom_call_target="tpu_custom_call" | custom-call | tf_op jit(solution)/shard_map/pallas_call | solution.py:632
Async XLA Ops:
  0.6 1.2 %copy-start = (bf16[64,8192]{1,0:T(8,128)(2,1)S(1)}, bf16[64,8192]{1,0:T(8,128)(2,1)}, u32[]{:S(2)}) copy-start(bf16[64,8192]{1,0:T(8,128)(2,1)} %strain_ref.1) | copy-start | bytes 3145732
  1.9 0.8 %copy-start.1 = (f32[64,64]{1,0:T(8,128)S(1)}, f32[64,64]{1,0:T(8,128)}, u32[]{:S(2)}) copy-start(f32[64,64]{1,0:T(8,128)} %taps_ref.1) | copy-start | bytes 49156

commit v5 on v4

--- a/solution.py
+++ b/solution.py
@@ -238,8 +238,8 @@
 
 def front_kernel(
     near, strain_ref, taps_ref, hankel_ref, out_ref,
-    rim, phase_ref, both, total, from_near, own, from_far, full,
-    rim_sem, both_sem, near_sem, far_sem, spread_sem, all_sem, hand_sem,
+    rim, phase_ref, both, total, from_near, own, from_far, head,
+    rim_sem, both_sem, near_sem, far_sem, spread_sem, all_sem, hand_sem, head_sem,
 ):
     tm, chan = lax.axis_index("tm"), lax.axis_index("chan")
     count_tm = lax.axis_size("tm")
@@ -283,9 +283,13 @@
     for partner in partners:
         pl.semaphore_signal(barrier, inc=1, device_id=partner, device_id_type=MESH)
     select = selection()
-    for g in range(groups):
-        here = slice(g * width, (g + 1) * width)
-        phases(jnp.dot(strain_ref[:, here], select, preferred_element_type=jnp.float32), phase_ref, g)
+    stack = jnp.concatenate([strain_ref[:, g * width : (g + 1) * width] for g in range(groups)], axis=0)
+    for n in range(0, STRIDE, 2):
+        part = jnp.dot(stack, select[:, n * LANES : (n + 2) * LANES], preferred_element_type=jnp.float32)
+        for g in range(groups):
+            here = slice(g * LANES, (g + 1) * LANES)
+            for s in range(2):
+                phase_ref[n + s, :, here] = part[g * channels : (g + 1) * channels, s * LANES : (s + 1) * LANES]
     pl.semaphore_wait(barrier, len(partners))
     rim_step = copy(strain_ref.at[:, :LANES], rim, rim_sem, 0, before)
     inner, edge = slice(0, groups * LANES), slice((groups - 1) * LANES, (groups + 1) * LANES)
@@ -321,20 +325,34 @@
             (((1,), (1,)), ((), ())),
             preferred_element_type=jnp.float32,
         )
-    head = jnp.concatenate([both[0, :, :LANES], both[1, :, :LANES]], axis=0).astype(jnp.float32).T
-    head = jnp.where(chan == 0, head[:8], head[8:16])
-
     half = LAGS * size // 2
     piece = half // near
     sub = piece // far
-    pitch = sub + 8
 
     def at_full(core_of, spot_of, place_of, rows):
-        return block(((core_of * near + spot_of) * far + place_of) * pitch, rows)
+        return block(((core_of * near + spot_of) * far + place_of) * sub, rows)
 
     steps = []
     for d in range(1, near):
         steps.append(copy(total.at[block(near_of(d) * piece, piece)], from_near.at[d - 1], near_sem, d - 1, near_id(d)))
+
+    def head_step(d):
+        return pltpu.make_async_remote_copy(
+            src_ref=head,
+            dst_ref=head,
+            send_sem=head_sem.at[d],
+            recv_sem=head_sem.at[0],
+            device_id={"tm": lax.rem(tm + d, count_tm)},
+            device_id_type=MESH,
+        )
+
+    @pl.when(tm == 0)
+    def _():
+        both_heads = jnp.concatenate([both[0, :, :LANES], both[1, :, :LANES]], axis=0).astype(jnp.float32)
+        head[...] = both_heads.T[: head.shape[0]]
+        for d in range(1, count_tm):
+            head_step(d).start()
+
     value = total[block(spot * piece, piece)]
     for d in range(1, near):
         steps[d - 1].wait()
@@ -348,28 +366,34 @@
         for d in range(1, far):
             steps[d - 1].wait()
             value += from_far[d - 1]
-    here = at_full(chan, spot, place, pitch)
-    full[here] = jnp.concatenate([value, head], axis=0)
+    here = at_full(chan, spot, place, sub)
+    out_ref[here] = value
     steps = []
     for d in range(1, far):
-        steps.append(copy(full.at[here], full.at[here], spread_sem, d - 1, far_id(d)))
+        steps.append(copy(out_ref.at[here], out_ref.at[here], spread_sem, d - 1, far_id(d)))
     for step in steps:
         step.wait()
-    here = at_full(chan, spot, 0, far * pitch)
+    here = at_full(chan, spot, 0, piece)
     steps = []
     for d in range(1, near):
-        steps.append(copy(full.at[here], full.at[here], all_sem, d - 1, near_id(d)))
+        steps.append(copy(out_ref.at[here], out_ref.at[here], all_sem, d - 1, near_id(d)))
+
+    @pl.when(tm == 0)
+    def _():
+        for d in range(1, count_tm):
+            head_step(d).wait_send()
+
+    @pl.when(tm != 0)
+    def _():
+        head_step(1).wait_recv()
+
+    ends = jnp.concatenate([head[...], jnp.zeros((size - head.shape[0], size), jnp.float32)], axis=0)
+    out_ref[LAGS * size :, :] = ends.T
     for step in steps:
         step.wait()
-    here = at_full(chan, 0, 0, near * far * pitch)
-    step = copy(full.at[here], full.at[here], hand_sem, 0, core)
+    here = block(chan * half, half)
+    step = copy(out_ref.at[here], out_ref.at[here], hand_sem, 0, core)
     step.wait()
-    for i in range(2 * near * far):
-        out_ref[i * sub : (i + 1) * sub, :] = full[i * pitch : i * pitch + sub, :]
-    there = near * far * pitch
-    ends = [full[sub : sub + 8, :], full[there + sub : there + sub + 8, :]]
-    ends.append(jnp.zeros((size - 16, size), jnp.float32))
-    out_ref[LAGS * size :, :] = jnp.concatenate(ends, axis=0).T
 
 
 def front(strain, taps):
@@ -401,7 +425,7 @@
             pltpu.VMEM((near - 1, piece, size), dtype),
             pltpu.VMEM((piece, size), dtype),
             pltpu.VMEM((farther, sub, size), dtype),
-            pltpu.VMEM(((sub + 8) * 2 * near * far, size), dtype),
+            pltpu.VMEM((2 * LAGS, size), dtype),
             dma((2, 1)),
             dma((2, 1)),
             dma((2, near - 1)),
@@ -409,6 +433,7 @@
             dma((2, farther)),
             dma((2, near - 1)),
             dma((2, 1)),
+            dma((tm,)),
         ],
         compiler_params=pltpu.CompilerParams(
             collective_id=1, has_side_effects=True, vmem_limit_bytes=40 * 2**20

time: 63.9 us -> 62.4 us (0.977)
  Pallas kernels: 61.1 us -> 59.5 us
    pallas_call x1, Pallas kernels: 31.8 us -> 30.4 us  [front(): pl.pallas_call(functools.partial(front_kernel, near), out_shape=(jax.Shap...]
where the time goes in v5:
time: 62.4 us; the launch traced here: 62.1 us
  Pallas kernels  59.5 us (95%)
  local copies, waits for them, and re-layouts  1.98 us (3%)
  between operations  0.65 us (1%)
    pallas_call x1, Pallas kernels, front(): pl.pallas_call(functools.partial(front_kernel, near), out_shape=(jax.Shap...  30.4 us
    pallas_call x1, Pallas kernels, whiten(): pl.pallas_call(functools.partial(whiten_kernel, rows_all), out_shape=(jax...  29.1 us
    unnamed x4, local copies, waits for them, and re-layouts  1.98 us

profile of v5, /device:TPU:9, one launch (start us, length us, event | category | flops | bytes accessed | tf_op | source)
XLA Modules:
  0.0 62.1 jit_solution(16380174659083775287)
XLA Ops:
  0.6 0.0 copy-start
  0.6 1.2 %copy-done = bf16[64,8192]{1,0:T(8,128)(2,1)S(1)} copy-done((bf16[64,8192]{1,0:T(8,128)(2,1)S(1)}, bf16[64,8192]{1,0:T(8,128)(2,1)}, u32[]{:S(2)}) %copy-start) | copy-done | bytes 1048600
  1.9 0.0 copy-start.1
  1.9 0.8 %copy-done.1 = f32[64,64]{1,0:T(8,128)S(1)} copy-done((f32[64,64]{1,0:T(8,128)S(1)}, f32[64,64]{1,0:T(8,128)}, u32[]{:S(2)}) %copy-start.1) | copy-done | bytes 16408
  2.6 30.4 %shard_map.41 = (bf16[1024,512]{1,0:T(8,128)(2,1)S(1)}, f32[1152,128]{1,0:T(8,128)S(1)}) custom-call(bf16[64,8192]{1,0:T(8,128)(2,1)S(1)} %copy-done, f32[64,64]{1,0:T(8,128)S(1)} %copy-done.1), custom_call_target="tpu_custom_call" | custom-call | tf_op jit(solution)/shard_map/pallas_call | solution.py:412
  33.1 29.1 %shard_map.42 = (f32[32,1024]{1,0:T(8,128)}, bf16[1024,512]{1,0:T(8,128)(2,1)}) custom-call(f32[1152,128]{1,0:T(8,128)S(1)} %get-tuple-element.4.sums_ref, bf16[1024,512]{1,0:T(8,128)(2,1)S(1)} %get-tuple-element.5.hankel_ref), custom_call_target="tpu_custom_call" | custom-call | tf_op jit(solution)/shard_map/pallas_call | solution.py:657
Async XLA Ops:
  0.6 1.2 %copy-start = (bf16[64,8192]{1,0:T(8,128)(2,1)S(1)}, bf16[64,8192]{1,0:T(8,128)(2,1)}, u32[]{:S(2)}) copy-start(bf16[64,8192]{1,0:T(8,128)(2,1)} %strain_ref.1) | copy-start | bytes 3145732
  1.9 0.8 %copy-start.1 = (f32[64,64]{1,0:T(8,128)S(1)}, f32[64,64]{1,0:T(8,128)}, u32[]{:S(2)}) copy-start(f32[64,64]{1,0:T(8,128)} %taps_ref.1) | copy-start | bytes 49156

commit v6 on v5

--- a/solution.py
+++ b/solution.py
@@ -237,9 +237,9 @@
 
 
 def front_kernel(
-    near, strain_ref, taps_ref, hankel_ref, out_ref,
-    rim, phase_ref, both, total, from_near, own, from_far, head,
-    rim_sem, both_sem, near_sem, far_sem, spread_sem, all_sem, hand_sem, head_sem,
+    near, strain_from, taps_ref, hankel_ref, out_ref,
+    strain_ref, rim, phase_ref, both, total, from_near, own, from_far, head,
+    load_sem, rim_sem, both_sem, near_sem, far_sem, spread_sem, all_sem, hand_sem, head_sem,
 ):
     tm, chan = lax.axis_index("tm"), lax.axis_index("chan")
     count_tm = lax.axis_size("tm")
@@ -278,11 +278,14 @@
     channels, samples = strain_ref.shape
     width = STRIDE * LANES
     groups = samples // width
+    load = pltpu.make_async_copy(strain_from, strain_ref, load_sem)
+    load.start()
     barrier = pltpu.get_barrier_semaphore()
     partners = [before, behind, core] + [near_id(d) for d in range(1, near)] + [far_id(d) for d in range(1, far)]
     for partner in partners:
         pl.semaphore_signal(barrier, inc=1, device_id=partner, device_id_type=MESH)
     select = selection()
+    load.wait()
     stack = jnp.concatenate([strain_ref[:, g * width : (g + 1) * width] for g in range(groups)], axis=0)
     for n in range(0, STRIDE, 2):
         part = jnp.dot(stack, select[:, n * LANES : (n + 2) * LANES], preferred_element_type=jnp.float32)
@@ -415,9 +418,10 @@
             jax.ShapeDtypeStruct((LAGS * size, samples // STRIDE // 2), jnp.bfloat16),
             jax.ShapeDtypeStruct(((LAGS + 1) * size, size), dtype),
         ),
-        in_specs=[VMEM, VMEM],
+        in_specs=[pl.BlockSpec(memory_space=pl.ANY), VMEM],
         out_specs=(VMEM, VMEM),
         scratch_shapes=[
+            pltpu.VMEM((channels, samples), jnp.bfloat16),
             pltpu.VMEM((channels, LANES), jnp.bfloat16),
             pltpu.VMEM((STRIDE, channels, span), dtype),
             pltpu.VMEM((2, channels, span), jnp.bfloat16),
@@ -426,6 +430,7 @@
             pltpu.VMEM((piece, size), dtype),
             pltpu.VMEM((farther, sub, size), dtype),
             pltpu.VMEM((2 * LAGS, size), dtype),
+            pltpu.SemaphoreType.DMA,
             dma((2, 1)),
             dma((2, 1)),
             dma((2, near - 1)),
@@ -436,7 +441,7 @@
             dma((tm,)),
         ],
         compiler_params=pltpu.CompilerParams(
-            collective_id=1, has_side_effects=True, vmem_limit_bytes=40 * 2**20
+            collective_id=1, has_side_effects=True, vmem_limit_bytes=52 * 2**20
         ),
     )(strain, taps)
 

time: 62.4 us -> 61.2 us (0.981)
  local copies, waits for them, and re-layouts: 1.98 us -> 0.75 us
    unnamed x4 -> x2, local copies, waits for them, and re-layouts: 1.98 us -> 0.75 us
where the time goes in v6:
time: 61.2 us; the launch traced here: 61 us
  Pallas kernels  59.6 us (97%)
  local copies, waits for them, and re-layouts  0.75 us (1%)
  between operations  0.65 us (1%)
    pallas_call x1, Pallas kernels, front(): pl.pallas_call(functools.partial(front_kernel, near), out_shape=(jax.Shap...  30.5 us
    pallas_call x1, Pallas kernels, whiten(): pl.pallas_call(functools.partial(whiten_kernel, rows_all), out_shape=(jax...  29.1 us

profile of v6, /device:TPU:9, one launch (start us, length us, event | category | flops | bytes accessed | tf_op | source)
XLA Modules:
  0.0 61.0 jit_solution(11249061787670023146)
XLA Ops:
  0.6 0.0 copy-start
  0.6 0.7 %copy-done = f32[64,64]{1,0:T(8,128)S(1)} copy-done((f32[64,64]{1,0:T(8,128)S(1)}, f32[64,64]{1,0:T(8,128)}, u32[]{:S(2)}) %copy-start) | copy-done | bytes 16408
  1.4 30.5 %shard_map.41 = (bf16[1024,512]{1,0:T(8,128)(2,1)S(1)}, f32[1152,128]{1,0:T(8,128)S(1)}) custom-call(bf16[64,8192]{1,0:T(8,128)(2,1)} %strain_from.1, f32[64,64]{1,0:T(8,128)S(1)} %copy-done), custom_call_target="tpu_custom_call" | custom-call | tf_op jit(solution)/shard_map/pallas_call | solution.py:415
  31.9 29.1 %shard_map.42 = (f32[32,1024]{1,0:T(8,128)}, bf16[1024,512]{1,0:T(8,128)(2,1)}) custom-call(f32[1152,128]{1,0:T(8,128)S(1)} %get-tuple-element.4.sums_ref, bf16[1024,512]{1,0:T(8,128)(2,1)S(1)} %get-tuple-element.5.hankel_ref), custom_call_target="tpu_custom_call" | custom-call | tf_op jit(solution)/shard_map/pallas_call | solution.py:662
Async XLA Ops:
  0.6 0.8 %copy-start = (f32[64,64]{1,0:T(8,128)S(1)}, f32[64,64]{1,0:T(8,128)}, u32[]{:S(2)}) copy-start(f32[64,64]{1,0:T(8,128)} %taps_ref.1) | copy-start | bytes 49156

commit v7 on v6

--- a/solution.py
+++ b/solution.py
@@ -238,7 +238,7 @@
 
 def front_kernel(
     near, strain_from, taps_ref, hankel_ref, out_ref,
-    strain_ref, rim, phase_ref, both, total, from_near, own, from_far, head,
+    strain_ref, rim, phase_ref, both, lags_ref, total, from_near, own, from_far, head,
     load_sem, rim_sem, both_sem, near_sem, far_sem, spread_sem, all_sem, hand_sem, head_sem,
 ):
     tm, chan = lax.axis_index("tm"), lax.axis_index("chan")
@@ -281,7 +281,9 @@
     load = pltpu.make_async_copy(strain_from, strain_ref, load_sem)
     load.start()
     barrier = pltpu.get_barrier_semaphore()
-    partners = [before, behind, core] + [near_id(d) for d in range(1, near)] + [far_id(d) for d in range(1, far)]
+    partners = [core] + [near_id(d) for d in range(1, near)] + [far_id(d) for d in range(1, far)]
+    if far > 1:
+        partners += [before, behind]
     for partner in partners:
         pl.semaphore_signal(barrier, inc=1, device_id=partner, device_id_type=MESH)
     select = selection()
@@ -304,27 +306,34 @@
     for c in range(0, channels, 16):
         both[chan, c : c + 16, edge] = taps_applied(slice(c, c + 16), edge, taps_ref, phase_ref)
     step = copy(both.at[chan], both.at[chan], both_sem, 0, core)
-    step.wait()
-
     size = 2 * channels
     count = hankel_ref.shape[1]
-    span = count + LANES
     start = pl.multiple_of(chan * count, LANES)
-    window = jnp.concatenate([both[0, :, pl.ds(start, span)], both[1, :, pl.ds(start, span)]], axis=0)
-    window = window.astype(jnp.float32)
-    for i in range(LAGS):
-        moved = window if i == 0 else pltpu.roll(window, span - i, 1)
-        hankel_ref[i * size : (i + 1) * size, :] = moved[:, :count].astype(jnp.bfloat16)
-    rows = jnp.concatenate([both[0], both[1]], axis=0).astype(jnp.float32)
-    span = rows.shape[1]
-    keep = lax.broadcasted_iota(jnp.int32, (size, 2 * count), 1) >= jnp.where(tm == 0, LAGS - 1, 0)
-    left = jnp.where(keep, rows[:, : 2 * count], 0.0).astype(jnp.bfloat16)
-    first = jnp.where(chan == 0, rows, pltpu.roll(rows, span - LAGS // 2, 1))
+
+    def spread(part):
+        span = count + LANES
+        window = both[part, :, pl.ds(start, span)].astype(jnp.float32)
+        for i in range(LAGS):
+            moved = window if i == 0 else pltpu.roll(window, span - i, 1)
+            there = pl.ds(pl.multiple_of(i * size + part * channels, channels), channels)
+            hankel_ref[there, :] = moved[:, :count].astype(jnp.bfloat16)
+        rows = both[part].astype(jnp.float32)
+        span = rows.shape[1]
+        keep = lax.broadcasted_iota(jnp.int32, (channels, 2 * count), 1) >= jnp.where(tm == 0, LAGS - 1, 0)
+        there = pl.ds(pl.multiple_of(part * channels, channels), channels)
+        lags_ref[LAGS // 2, there, :] = jnp.where(keep, rows[:, : 2 * count], 0.0).astype(jnp.bfloat16)
+        first = jnp.where(chan == 0, rows, pltpu.roll(rows, span - LAGS // 2, 1))
+        for i in range(LAGS // 2):
+            moved = first if i == 0 else pltpu.roll(first, span - i, 1)
+            lags_ref[i, there, :] = moved[:, : 2 * count].astype(jnp.bfloat16)
+
+    spread(chan)
+    step.wait()
+    spread(1 - chan)
     for i in range(LAGS // 2):
-        moved = first if i == 0 else pltpu.roll(first, span - i, 1)
         total[i * size : (i + 1) * size, :] = lax.dot_general(
-            left,
-            moved[:, : 2 * count].astype(jnp.bfloat16),
+            lags_ref[LAGS // 2],
+            lags_ref[i],
             (((1,), (1,)), ((), ())),
             preferred_element_type=jnp.float32,
         )
@@ -425,6 +434,7 @@
             pltpu.VMEM((channels, LANES), jnp.bfloat16),
             pltpu.VMEM((STRIDE, channels, span), dtype),
             pltpu.VMEM((2, channels, span), jnp.bfloat16),
+            pltpu.VMEM((LAGS // 2 + 1, size, samples // STRIDE), jnp.bfloat16),
             pltpu.VMEM((half, size), dtype),
             pltpu.VMEM((near - 1, piece, size), dtype),
             pltpu.VMEM((piece, size), dtype),
@@ -543,7 +553,7 @@
 
 
 def whiten_kernel(
-    rows_all, sums_ref, hankel_ref, factor_ref, white_ref, work_ref, pairs_ref, turned_ref, part_ref, block_ref
+    rows_all, sums_ref, hankel_ref, factor_ref, white_ref, work_ref, pairs_ref, turned_ref, part_ref, block_ref, down_ref
 ):
     columns, count = hankel_ref.shape
     channels = columns // LAGS
@@ -574,10 +584,8 @@
             if i + j == 0:
                 block_ref[...] = part
             work_ref[i * size : (i + 1) * size, (i + j) * size : (i + j + 1) * size] = part
-        work_ref[i * channels : (i + 1) * channels, columns:] = (
-            hankel_ref[i * channels : (i + 1) * channels, :].astype(jnp.float32) * down
-        )
     near = columns // 2
+    down_ref[...] = jnp.broadcast_to(down, down_ref.shape)
     turned_ref[...] = jnp.zeros(turned_ref.shape, jnp.bfloat16)
     pairs_ref[:columns] = jnp.zeros((columns, total), jnp.bfloat16)
 
@@ -610,7 +618,11 @@
 
         def prepare(n):
             here = slice(n, n + width)
-            high, mid = halves(work_ref[mine, here] - product(2 * depth, here))
+            if n < columns:
+                whole = work_ref[mine, here]
+            else:
+                whole = hankel_ref[mine, n - columns : n - columns + width].astype(jnp.float32) * down_ref[...]
+            high, mid = halves(whole - product(2 * depth, here))
             part_ref[:size, here] = high
             part_ref[size:, here] = mid
 
@@ -668,11 +680,12 @@
         in_specs=[VMEM, VMEM],
         out_specs=(VMEM, VMEM),
         scratch_shapes=[
-            pltpu.VMEM((columns, columns + count), jnp.float32),
+            pltpu.VMEM((columns, columns), jnp.float32),
             pltpu.VMEM((2 * columns, columns + count), jnp.bfloat16),
             pltpu.VMEM((2 * size, 2 * columns), jnp.bfloat16),
             pltpu.VMEM((2 * size, columns + count), jnp.bfloat16),
             pltpu.VMEM((size, size), jnp.float32),
+            pltpu.VMEM((size, 2 * size), jnp.float32),
         ],
         compiler_params=pltpu.CompilerParams(vmem_limit_bytes=48 * 2**20),
     )(sums, hankel)

time: 61.2 us -> 61.1 us (level)
  no operation moved by 1% of the time
where the time goes in v7:
time: 61.1 us; the launch traced here: 60.4 us
  Pallas kernels  59 us (97%)
  local copies, waits for them, and re-layouts  0.75 us (1%)
  between operations  0.65 us (1%)
    pallas_call x1, Pallas kernels, front(): pl.pallas_call(functools.partial(front_kernel, near), out_shape=(jax.Shap...  30.1 us
    pallas_call x1, Pallas kernels, whiten(): pl.pallas_call(functools.partial(whiten_kernel, rows_all), out_shape=(jax...  29 us

profile of v7, /device:TPU:9, one launch (start us, length us, event | category | flops | bytes accessed | tf_op | source)
XLA Modules:
  0.0 60.4 jit_solution(10885970908127597612)
XLA Ops:
  0.6 0.0 copy-start
  0.6 0.7 %copy-done = f32[64,64]{1,0:T(8,128)S(1)} copy-done((f32[64,64]{1,0:T(8,128)S(1)}, f32[64,64]{1,0:T(8,128)}, u32[]{:S(2)}) %copy-start) | copy-done | bytes 16408
  1.4 30.1 %shard_map.41 = (bf16[1024,512]{1,0:T(8,128)(2,1)S(1)}, f32[1152,128]{1,0:T(8,128)S(1)}) custom-call(bf16[64,8192]{1,0:T(8,128)(2,1)} %strain_from.1, f32[64,64]{1,0:T(8,128)S(1)} %copy-done), custom_call_target="tpu_custom_call" | custom-call | tf_op jit(solution)/shard_map/pallas_call | solution.py:424
  31.4 29.0 %shard_map.42 = (f32[32,1024]{1,0:T(8,128)}, bf16[1024,512]{1,0:T(8,128)(2,1)}) custom-call(f32[1152,128]{1,0:T(8,128)S(1)} %get-tuple-element.4.sums_ref, bf16[1024,512]{1,0:T(8,128)(2,1)S(1)} %get-tuple-element.5.hankel_ref), custom_call_target="tpu_custom_call" | custom-call | tf_op jit(solution)/shard_map/pallas_call | solution.py:674
Async XLA Ops:
  0.6 0.8 %copy-start = (f32[64,64]{1,0:T(8,128)S(1)}, f32[64,64]{1,0:T(8,128)}, u32[]{:S(2)}) copy-start(f32[64,64]{1,0:T(8,128)} %taps_ref.1) | copy-start | bytes 49156

commit v8 on v7

--- a/solution.py
+++ b/solution.py
@@ -656,8 +656,8 @@
                 white_ref[mine, n - columns : n - columns + width] = solved.astype(jnp.bfloat16)
         return 0
 
-    lax.fori_loop(0, LAGS // 2, functools.partial(step, near - size, 0), 0)
-    lax.fori_loop(LAGS // 2, LAGS, functools.partial(step, columns - size, near), 0)
+    for k in range(0, LAGS, 2):
+        lax.fori_loop(k, k + 2, functools.partial(step, (k + 1) * size, k * size), 0)
     kept = factor_ref.shape[0]
     me = lax.axis_index("tm") * lax.axis_size("chan") + lax.axis_index("chan")
     first_row = pl.multiple_of(me * (columns // (lax.axis_size("tm") * lax.axis_size("chan"))) // kept * kept, kept)

time: 61.1 us -> 60.2 us (0.985)
  Pallas kernels: 59 us -> 58.2 us
    pallas_call x1, Pallas kernels: 29 us -> 28.1 us  [whiten(): pl.pallas_call(functools.partial(whiten_kernel, rows_all), out_shape=(jax...]
where the time goes in v8:
time: 60.2 us; the launch traced here: 59.6 us
  Pallas kernels  58.2 us (97%)
  local copies, waits for them, and re-layouts  0.75 us (1%)
  between operations  0.65 us (1%)
    pallas_call x1, Pallas kernels, front(): pl.pallas_call(functools.partial(front_kernel, near), out_shape=(jax.Shap...  30.1 us
    pallas_call x1, Pallas kernels, whiten(): pl.pallas_call(functools.partial(whiten_kernel, rows_all), out_shape=(jax...  28.1 us

profile of v8, /device:TPU:9, one launch (start us, length us, event | category | flops | bytes accessed | tf_op | source)
XLA Modules:
  0.0 59.6 jit_solution(1847217820207778074)
XLA Ops:
  0.6 0.0 copy-start
  0.6 0.7 %copy-done = f32[64,64]{1,0:T(8,128)S(1)} copy-done((f32[64,64]{1,0:T(8,128)S(1)}, f32[64,64]{1,0:T(8,128)}, u32[]{:S(2)}) %copy-start) | copy-done | bytes 16408
  1.4 30.1 %shard_map.41 = (bf16[1024,512]{1,0:T(8,128)(2,1)S(1)}, f32[1152,128]{1,0:T(8,128)S(1)}) custom-call(bf16[64,8192]{1,0:T(8,128)(2,1)} %strain_from.1, f32[64,64]{1,0:T(8,128)S(1)} %copy-done), custom_call_target="tpu_custom_call" | custom-call | tf_op jit(solution)/shard_map/pallas_call | solution.py:424
  31.4 28.1 %shard_map.42 = (f32[32,1024]{1,0:T(8,128)}, bf16[1024,512]{1,0:T(8,128)(2,1)}) custom-call(f32[1152,128]{1,0:T(8,128)S(1)} %get-tuple-element.4.sums_ref, bf16[1024,512]{1,0:T(8,128)(2,1)S(1)} %get-tuple-element.5.hankel_ref), custom_call_target="tpu_custom_call" | custom-call | tf_op jit(solution)/shard_map/pallas_call | solution.py:674
Async XLA Ops:
  0.6 0.8 %copy-start = (f32[64,64]{1,0:T(8,128)S(1)}, f32[64,64]{1,0:T(8,128)}, u32[]{:S(2)}) copy-start(f32[64,64]{1,0:T(8,128)} %taps_ref.1) | copy-start | bytes 49156

commit v9 on v8

--- a/solution.py
+++ b/solution.py
@@ -635,15 +635,17 @@
             seen.append(product(2 * depth, after))
 
         jobs = [functools.partial(prepare, n) for n in range(initial, total, width)]
-        jobs.append(look_ahead)
+        ends = depth == columns - size
+        if not ends:
+            jobs.append(look_ahead)
         inverse = factor_inverse(block_ref[...], jobs)
-        seen = work_ref[after, after] - seen[0]
-
         left = stacked(*halves(inverse))
-        high, mid = halves(small(left, part_ref[:, after]))
-        high_turned, mid_turned = high.T, mid.T
-        block_ref[...] = seen - small(stacked(high_turned, mid_turned), jnp.concatenate([high, mid], axis=0))
-        turn(k, high_turned, mid_turned)
+        if not ends:
+            high, mid = halves(small(left, part_ref[:, after]))
+            high_turned, mid_turned = high.T, mid.T
+            rest = work_ref[after, after] - seen[0]
+            block_ref[...] = rest - small(stacked(high_turned, mid_turned), jnp.concatenate([high, mid], axis=0))
+            turn(k, high_turned, mid_turned)
         for n in range(initial, total, width):
             here = slice(n, n + width)
             solved = small(left, part_ref[:, here])
@@ -656,8 +658,10 @@
                 white_ref[mine, n - columns : n - columns + width] = solved.astype(jnp.bfloat16)
         return 0
 
-    for k in range(0, LAGS, 2):
+    for k in range(0, LAGS - 2, 2):
         lax.fori_loop(k, k + 2, functools.partial(step, (k + 1) * size, k * size), 0)
+    for k in (LAGS - 2, LAGS - 1):
+        lax.fori_loop(k, k + 1, functools.partial(step, k * size, columns - 2 * size), 0)
     kept = factor_ref.shape[0]
     me = lax.axis_index("tm") * lax.axis_size("chan") + lax.axis_index("chan")
     first_row = pl.multiple_of(me * (columns // (lax.axis_size("tm") * lax.axis_size("chan"))) // kept * kept, kept)

time: 60.2 us -> 59.3 us (0.985)
  Pallas kernels: 58.2 us -> 57.2 us
    pallas_call x1, Pallas kernels: 28.1 us -> 27.2 us  [whiten(): pl.pallas_call(functools.partial(whiten_kernel, rows_all), out_shape=(jax...]
where the time goes in v9:
time: 59.3 us; the launch traced here: 58.6 us
  Pallas kernels  57.2 us (96%)
  local copies, waits for them, and re-layouts  0.75 us (1%)
  between operations  0.65 us (1%)
    pallas_call x1, Pallas kernels, front(): pl.pallas_call(functools.partial(front_kernel, near), out_shape=(jax.Shap...  30.1 us
    pallas_call x1, Pallas kernels, whiten(): pl.pallas_call(functools.partial(whiten_kernel, rows_all), out_shape=(jax...  27.2 us

profile of v9, /device:TPU:9, one launch (start us, length us, event | category | flops | bytes accessed | tf_op | source)
XLA Modules:
  0.0 58.6 jit_solution(7217711787739977603)
XLA Ops:
  0.6 0.0 copy-start
  0.6 0.7 %copy-done = f32[64,64]{1,0:T(8,128)S(1)} copy-done((f32[64,64]{1,0:T(8,128)S(1)}, f32[64,64]{1,0:T(8,128)}, u32[]{:S(2)}) %copy-start) | copy-done | bytes 16408
  1.4 30.1 %shard_map.41 = (bf16[1024,512]{1,0:T(8,128)(2,1)S(1)}, f32[1152,128]{1,0:T(8,128)S(1)}) custom-call(bf16[64,8192]{1,0:T(8,128)(2,1)} %strain_from.1, f32[64,64]{1,0:T(8,128)S(1)} %copy-done), custom_call_target="tpu_custom_call" | custom-call | tf_op jit(solution)/shard_map/pallas_call | solution.py:424
  31.4 27.2 %shard_map.42 = (f32[32,1024]{1,0:T(8,128)}, bf16[1024,512]{1,0:T(8,128)(2,1)}) custom-call(f32[1152,128]{1,0:T(8,128)S(1)} %get-tuple-element.4.sums_ref, bf16[1024,512]{1,0:T(8,128)(2,1)S(1)} %get-tuple-element.5.hankel_ref), custom_call_target="tpu_custom_call" | custom-call | tf_op jit(solution)/shard_map/pallas_call | solution.py:678
Async XLA Ops:
  0.6 0.8 %copy-start = (f32[64,64]{1,0:T(8,128)S(1)}, f32[64,64]{1,0:T(8,128)}, u32[]{:S(2)}) copy-start(f32[64,64]{1,0:T(8,128)} %taps_ref.1) | copy-start | bytes 49156
